TPU v7x, 128 devices: a whole 4x4x4 slice. The times are simulated.
128 devices in a mesh: ctx: 16 (over x_lo, z, core), head: 8 (over y, x_hi).
Axes of the slice: x: 4 (x_hi: 2, x_lo: 2; x = x_hi * 2 + x_lo), y: 4, z: 4, core: 2. Of those that a mesh axis runs over, the one named last changes fastest.
Arguments:
- states: bfloat16 [16384, 4096], P('ctx'), may hold values from -64 to 64
- seg_ids: int32 [16384], replicated, may hold values from 0 to 3, never falling along the last dimension, each value on 1 to 8192 neighbouring positions
- span_order: int32 [32], replicated, may hold values from 0 to 31, as said below
- w_query: bfloat16 [4096, 2048], P(None, 'head'), may hold values from -0.09375 to 0.09375
- w_key: bfloat16 [4096, 1024], P(None, 'head'), may hold values from -0.09375 to 0.09375
- w_value: bfloat16 [4096, 1024], P(None, 'head'), may hold values from -1.5 to 1.5
- w_out: bfloat16 [2048, 4096], P('head'), may hold values from -0.1875 to 0.1875
Outputs:
- block_out: bfloat16 [16384, 4096], P('ctx', 'head')
Inputs may be any that keep to these rules, and one draw needn't show every extreme that they name: `span_order`: each span of 512 positions stands in exactly one slot; the slots 2 d and 2 d + 1 of device d of ctx hold spans i and 31 - i for some i, in either order.
All inputs are finite; a program needn't handle non-finite values.
Results may differ from a plain program's by a relative error of at most 0.019.
Values may be sent and summed in bfloat16 or wider, within the bound.
No kernel may reach another device: no remote copies, remote signals or barrier semaphores. Data moves between devices by JAX's collectives and lax.ppermute only.
A program may use at most 128 MiB of HBM per device.

v0:
```python
import math

import jax
import jax.numpy as jnp
from jax import lax
from jax.sharding import PartitionSpec as P

HD = 128


rope_base = 500000.0
neg_large = -1e30
block_limit = 2048


def rotate(values, positions):
    middle = values.shape[-1] // 2
    frequency = rope_base ** (-jnp.arange(middle, dtype=jnp.float32) * 2.0 / values.shape[-1])
    angles = positions.astype(jnp.float32)[:, None] * frequency[None, :]
    cos_part = jnp.cos(angles)[:, None, :]
    sin_part = jnp.sin(angles)[:, None, :]
    first_half = values[..., :middle]
    second_half = values[..., middle:]
    return jnp.concatenate(
        [
            first_half * cos_part - second_half * sin_part,
            second_half * cos_part + first_half * sin_part,
        ],
        -1,
    )


def update(query_part, query_pos, query_seg, running, key_block, value_block, key_pos, key_seg):
    row_max, totals, accumulated = running
    scores = jnp.einsum("kgqd,tkd->kgqt", query_part, key_block, preferred_element_type=jnp.float32)
    allowed = (key_pos[None, :] <= query_pos[:, None]) & (key_seg[None, :] == query_seg[:, None])
    scores = jnp.where(allowed, scores, neg_large)
    new_max = jnp.maximum(row_max, jnp.max(scores, -1))
    weights = jnp.where(allowed, jnp.exp(scores - new_max[..., None]), 0.0)
    factor = jnp.exp(row_max - new_max)
    totals = totals * factor + jnp.sum(weights, -1)
    accumulated = accumulated * factor[..., None] + jnp.einsum(
        "kgqt,tkd->kgqd",
        weights.astype(jnp.bfloat16),
        value_block,
        preferred_element_type=jnp.float32,
    )
    return (new_max, totals, accumulated)


def per_device(states, seg_ids, span_order, w_query, w_key, w_value, w_out):
    local_rows = states.shape[0]
    span_rows = local_rows // 2
    kv_local = w_key.shape[1] // HD
    group_size = w_query.shape[1] // w_key.shape[1]
    device = lax.axis_index("ctx")
    my_spans = lax.dynamic_slice_in_dim(span_order, 2 * device, 2, 0)
    row_index = jnp.arange(local_rows, dtype=jnp.int32)
    positions = my_spans[row_index // span_rows] * span_rows + row_index % span_rows
    segments = seg_ids[positions]
    queries = jnp.dot(states, w_query, preferred_element_type=jnp.float32).reshape(
        local_rows, kv_local * group_size, HD
    )
    queries = (rotate(queries, positions) * HD ** (-0.5)).astype(jnp.bfloat16)
    queries = jnp.transpose(queries.reshape(local_rows, kv_local, group_size, HD), (1, 2, 0, 3))
    key_rows = jnp.dot(states, w_key, preferred_element_type=jnp.float32).reshape(
        local_rows, kv_local, HD
    )
    key_rows = rotate(key_rows, positions).astype(jnp.bfloat16).reshape(local_rows, kv_local * HD)
    value_rows = jnp.dot(states, w_value, preferred_element_type=jnp.float32).astype(jnp.bfloat16)
    initial = (
        jnp.full((kv_local, group_size, local_rows), neg_large, jnp.float32),
        jnp.zeros((kv_local, group_size, local_rows), jnp.float32),
        jnp.zeros((kv_local, group_size, local_rows, HD), jnp.float32),
    )
    key_piece = lax.all_gather(key_rows, "ctx", axis=0, tiled=True)
    value_piece = lax.all_gather(value_rows, "ctx", axis=0, tiled=True)
    piece_rows = key_piece.shape[0]
    block_rows = math.gcd(piece_rows, block_limit)

    def one_block(step_index, state):
        offset = step_index * block_rows
        key_block = lax.dynamic_slice_in_dim(key_piece, offset, block_rows, 0).reshape(
            block_rows, kv_local, HD
        )
        value_block = lax.dynamic_slice_in_dim(value_piece, offset, block_rows, 0).reshape(
            block_rows, kv_local, HD
        )
        global_rows = offset + jnp.arange(block_rows, dtype=jnp.int32)
        key_pos = span_order[global_rows // span_rows] * span_rows + global_rows % span_rows
        key_seg = seg_ids[key_pos]
        return update(queries, positions, segments, state, key_block, value_block, key_pos, key_seg)

    block_count = piece_rows // block_rows
    row_max, totals, accumulated = lax.fori_loop(0, block_count, one_block, initial)
    attended = (accumulated / totals[..., None]).astype(jnp.bfloat16)
    attended = jnp.transpose(attended, (2, 0, 1, 3)).reshape(local_rows, kv_local * group_size * HD)
    partial_value = jnp.dot(attended, w_out, preferred_element_type=jnp.float32)
    result = lax.psum_scatter(
        partial_value.astype(jnp.bfloat16), "head", scatter_dimension=1, tiled=True
    )
    return result


def solution(mesh):
    in_specs = (
        P("ctx", None),
        P(),
        P(),
        P(None, "head"),
        P(None, "head"),
        P(None, "head"),
        P("head", None),
    )
    out_specs = P("ctx", "head")
    return jax.shard_map(
        per_device, mesh=mesh, in_specs=in_specs, out_specs=out_specs, check_vma=False
    )
```

profile of v0, /device:TPU:0, one launch (start us, length us, event | category | flops | bytes accessed | tf_op | source)
XLA Modules:
  0.0 741.6 jit_solution(13589263713501576075)
XLA Ops:
  45.6 12.2 %all-gather.3.cloned.1.call-done = bf16[16384,128]{0,1:T(8,128)(2,1)} async-done(((bf16[1024,128]{0,1:T(8,128)(2,1)}), bf16[16384,128]{0,1:T(8,128)(2,1)}) %all-gather.3.cloned.1.call-update) | async-done | bytes 4194320 | tf_op jit(solution)/shard_map/all_gather | solution.py:76
  57.8 39.1 %all-gather.5.cloned.1.call-done = bf16[16384,128]{1,0:T(8,128)(2,1)} async-done(((bf16[1024,128]{1,0:T(8,128)(2,1)}), bf16[16384,128]{1,0:T(8,128)(2,1)}) %all-gather.5.cloned.1.call-update) | async-done | bytes 4194320 | tf_op jit(solution)/shard_map/all_gather | solution.py:77
  96.9 516.3 %while.20 = (s32[]{:T(128)}, f32[1,2,1024]{2,1,0:T(2,128)S(1)}, f32[1,2,1024]{2,1,0:T(2,128)S(1)}, f32[1,2,1024,128]{3,2,1,0:T(8,128)}, s32[32]{0:T(128)S(1)}, /...) while((s32[]{:T(128)}, f32[1,2,1024]{2,1,0:T(2,128)S(1)}, ...), condition=%wide.region_3.4_spmd.clone, body=%wide.region_0.3_spmd.clone.sunk | while | flops 2197273600 | bytes 138248928 | solution.py:95
  104.3 15.4 %fusion.85 = (s32[2048]{0:T(1024)S(1)}, s32[2048]{0:T(1024)S(1)}) fusion(s32[]{:T(128)S(6)} %mul.329, pred[2048]{0:T(1024)(128)(4,1)S(1)} %get-tuple-element.575, pred[2048]{0:T(1024)(128)(4,1)S(1)} %get-tuple-element.576, pred[2048]{0:T(1024)(128)(4,1)S(1)} %get-tuple-element.577, pred[2048]{0:T(1024)(128)(4,1)S(1)} %get-tuple-element.578, ...), kind=kLoop, calls=%fused_computation.66.clone.1 | loop fusion | flops 79872 | bytes 75880 | tf_op jit(solution)/shard_map/while/body/eval_jaxpr/add | solution.py:90
  119.8 11.8 %gather_fusion = s32[2048]{0:T(1024)S(1)} fusion(s32[16384]{0:T(1024)S(1)} %get-tuple-element.674, s32[2048]{0:T(1024)S(1)} %broadcast_clamp_fusion.3), kind=kCustom, calls=%fused_computation.clone.clone.1 | custom fusion | bytes 24576 | tf_op jit(solution)/shard_map/while/body/eval_jaxpr/gather | solution.py:91
  144.9 10.0 %fusion.89 = f32[1,2,1024,128]{3,2,1,0:T(8,128)} fusion(f32[2048,2,1024]{2,0,1:T(8,128)} %get-tuple-element.635, f32[2,1024]{1,0:T(2,128)S(1)} %bitcast.198, pred[1024,2048]{0,1:T(8,128)(4,1)} %compare_and_fusion.2, f32[1,2,1024,128]{3,2,1,0:T(8,128)} %get-tuple-element.656, bf16[16384,128]{1,0:T(8,128)(2,1)} %get-tuple-element.678, ...), kind=kOutput, calls=%fused_computation.12.clone.1 | convolution fusion | flops 1091305472 | bytes 21512196 | tf_op jit(solution)/shard_map/while/body/eval_jaxpr/kgqt,tkd->kgqd/dot_general | solution.py:42
  168.6 15.4 %fusion.85 = (s32[2048]{0:T(1024)S(1)}, s32[2048]{0:T(1024)S(1)}) fusion(s32[]{:T(128)S(6)} %mul.329, pred[2048]{0:T(1024)(128)(4,1)S(1)} %get-tuple-element.575, pred[2048]{0:T(1024)(128)(4,1)S(1)} %get-tuple-element.576, pred[2048]{0:T(1024)(128)(4,1)S(1)} %get-tuple-element.577, pred[2048]{0:T(1024)(128)(4,1)S(1)} %get-tuple-element.578, ...), kind=kLoop, calls=%fused_computation.66.clone.1 | loop fusion | flops 79872 | bytes 75880 | tf_op jit(solution)/shard_map/while/body/eval_jaxpr/add | solution.py:90
  184.0 11.8 %gather_fusion = s32[2048]{0:T(1024)S(1)} fusion(s32[16384]{0:T(1024)S(1)} %get-tuple-element.674, s32[2048]{0:T(1024)S(1)} %broadcast_clamp_fusion.3), kind=kCustom, calls=%fused_computation.clone.clone.1 | custom fusion | bytes 24576 | tf_op jit(solution)/shard_map/while/body/eval_jaxpr/gather | solution.py:91
  209.2 10.3 %fusion.89 = f32[1,2,1024,128]{3,2,1,0:T(8,128)} fusion(f32[2048,2,1024]{2,0,1:T(8,128)} %get-tuple-element.635, f32[2,1024]{1,0:T(2,128)S(1)} %bitcast.198, pred[1024,2048]{0,1:T(8,128)(4,1)} %compare_and_fusion.2, f32[1,2,1024,128]{3,2,1,0:T(8,128)} %get-tuple-element.656, bf16[16384,128]{1,0:T(8,128)(2,1)} %get-tuple-element.678, ...), kind=kOutput, calls=%fused_computation.12.clone.1 | convolution fusion | flops 1091305472 | bytes 21512196 | tf_op jit(solution)/shard_map/while/body/eval_jaxpr/kgqt,tkd->kgqd/dot_general | solution.py:42
  233.1 15.4 %fusion.85 = (s32[2048]{0:T(1024)S(1)}, s32[2048]{0:T(1024)S(1)}) fusion(s32[]{:T(128)S(6)} %mul.329, pred[2048]{0:T(1024)(128)(4,1)S(1)} %get-tuple-element.575, pred[2048]{0:T(1024)(128)(4,1)S(1)} %get-tuple-element.576, pred[2048]{0:T(1024)(128)(4,1)S(1)} %get-tuple-element.577, pred[2048]{0:T(1024)(128)(4,1)S(1)} %get-tuple-element.578, ...), kind=kLoop, calls=%fused_computation.66.clone.1 | loop fusion | flops 79872 | bytes 75880 | tf_op jit(solution)/shard_map/while/body/eval_jaxpr/add | solution.py:90
  248.6 11.8 %gather_fusion = s32[2048]{0:T(1024)S(1)} fusion(s32[16384]{0:T(1024)S(1)} %get-tuple-element.674, s32[2048]{0:T(1024)S(1)} %broadcast_clamp_fusion.3), kind=kCustom, calls=%fused_computation.clone.clone.1 | custom fusion | bytes 24576 | tf_op jit(solution)/shard_map/while/body/eval_jaxpr/gather | solution.py:91
  273.7 10.2 %fusion.89 = f32[1,2,1024,128]{3,2,1,0:T(8,128)} fusion(f32[2048,2,1024]{2,0,1:T(8,128)} %get-tuple-element.635, f32[2,1024]{1,0:T(2,128)S(1)} %bitcast.198, pred[1024,2048]{0,1:T(8,128)(4,1)} %compare_and_fusion.2, f32[1,2,1024,128]{3,2,1,0:T(8,128)} %get-tuple-element.656, bf16[16384,128]{1,0:T(8,128)(2,1)} %get-tuple-element.678, ...), kind=kOutput, calls=%fused_computation.12.clone.1 | convolution fusion | flops 1091305472 | bytes 21512196 | tf_op jit(solution)/shard_map/while/body/eval_jaxpr/kgqt,tkd->kgqd/dot_general | solution.py:42
  297.7 15.4 %fusion.85 = (s32[2048]{0:T(1024)S(1)}, s32[2048]{0:T(1024)S(1)}) fusion(s32[]{:T(128)S(6)} %mul.329, pred[2048]{0:T(1024)(128)(4,1)S(1)} %get-tuple-element.575, pred[2048]{0:T(1024)(128)(4,1)S(1)} %get-tuple-element.576, pred[2048]{0:T(1024)(128)(4,1)S(1)} %get-tuple-element.577, pred[2048]{0:T(1024)(128)(4,1)S(1)} %get-tuple-element.578, ...), kind=kLoop, calls=%fused_computation.66.clone.1 | loop fusion | flops 79872 | bytes 75880 | tf_op jit(solution)/shard_map/while/body/eval_jaxpr/add | solution.py:90
  313.1 11.8 %gather_fusion = s32[2048]{0:T(1024)S(1)} fusion(s32[16384]{0:T(1024)S(1)} %get-tuple-element.674, s32[2048]{0:T(1024)S(1)} %broadcast_clamp_fusion.3), kind=kCustom, calls=%fused_computation.clone.clone.1 | custom fusion | bytes 24576 | tf_op jit(solution)/shard_map/while/body/eval_jaxpr/gather | solution.py:91
  338.3 10.2 %fusion.89 = f32[1,2,1024,128]{3,2,1,0:T(8,128)} fusion(f32[2048,2,1024]{2,0,1:T(8,128)} %get-tuple-element.635, f32[2,1024]{1,0:T(2,128)S(1)} %bitcast.198, pred[1024,2048]{0,1:T(8,128)(4,1)} %compare_and_fusion.2, f32[1,2,1024,128]{3,2,1,0:T(8,128)} %get-tuple-element.656, bf16[16384,128]{1,0:T(8,128)(2,1)} %get-tuple-element.678, ...), kind=kOutput, calls=%fused_computation.12.clone.1 | convolution fusion | flops 1091305472 | bytes 21512196 | tf_op jit(solution)/shard_map/while/body/eval_jaxpr/kgqt,tkd->kgqd/dot_general | solution.py:42
  362.2 15.4 %fusion.85 = (s32[2048]{0:T(1024)S(1)}, s32[2048]{0:T(1024)S(1)}) fusion(s32[]{:T(128)S(6)} %mul.329, pred[2048]{0:T(1024)(128)(4,1)S(1)} %get-tuple-element.575, pred[2048]{0:T(1024)(128)(4,1)S(1)} %get-tuple-element.576, pred[2048]{0:T(1024)(128)(4,1)S(1)} %get-tuple-element.577, pred[2048]{0:T(1024)(128)(4,1)S(1)} %get-tuple-element.578, ...), kind=kLoop, calls=%fused_computation.66.clone.1 | loop fusion | flops 79872 | bytes 75880 | tf_op jit(solution)/shard_map/while/body/eval_jaxpr/add | solution.py:90
  377.7 11.8 %gather_fusion = s32[2048]{0:T(1024)S(1)} fusion(s32[16384]{0:T(1024)S(1)} %get-tuple-element.674, s32[2048]{0:T(1024)S(1)} %broadcast_clamp_fusion.3), kind=kCustom, calls=%fused_computation.clone.clone.1 | custom fusion | bytes 24576 | tf_op jit(solution)/shard_map/while/body/eval_jaxpr/gather | solution.py:91
  394.0 8.8 %fusion.86 = (f32[2,1024]{1,0:T(2,128)S(1)}, f32[2048,2,1024]{2,0,1:T(8,128)}) fusion(pred[1024,2048]{0,1:T(8,128)(4,1)} %compare_and_fusion.2, bf16[1,2,1024,128]{3,2,1,0:T(8,128)(2,1)S(1)} %get-tuple-element.677, bf16[16384,128]{0,1:T(8,128)(2,1)} %get-tuple-element.676, s32[]{:T(128)S(6)} %select_n.474), kind=kOutput, calls=%fused_computation.5.clone.1 | convolution fusion | flops 1082128384 | bytes 19931140 | tf_op jit(solution)/shard_map/while/body/eval_jaxpr/kgqd,tkd->kgqt/dot_general | solution.py:35
  402.9 10.2 %fusion.89 = f32[1,2,1024,128]{3,2,1,0:T(8,128)} fusion(f32[2048,2,1024]{2,0,1:T(8,128)} %get-tuple-element.635, f32[2,1024]{1,0:T(2,128)S(1)} %bitcast.198, pred[1024,2048]{0,1:T(8,128)(4,1)} %compare_and_fusion.2, f32[1,2,1024,128]{3,2,1,0:T(8,128)} %get-tuple-element.656, bf16[16384,128]{1,0:T(8,128)(2,1)} %get-tuple-element.678, ...), kind=kOutput, calls=%fused_computation.12.clone.1 | convolution fusion | flops 1091305472 | bytes 21512196 | tf_op jit(solution)/shard_map/while/body/eval_jaxpr/kgqt,tkd->kgqd/dot_general | solution.py:42
  426.8 15.4 %fusion.85 = (s32[2048]{0:T(1024)S(1)}, s32[2048]{0:T(1024)S(1)}) fusion(s32[]{:T(128)S(6)} %mul.329, pred[2048]{0:T(1024)(128)(4,1)S(1)} %get-tuple-element.575, pred[2048]{0:T(1024)(128)(4,1)S(1)} %get-tuple-element.576, pred[2048]{0:T(1024)(128)(4,1)S(1)} %get-tuple-element.577, pred[2048]{0:T(1024)(128)(4,1)S(1)} %get-tuple-element.578, ...), kind=kLoop, calls=%fused_computation.66.clone.1 | loop fusion | flops 79872 | bytes 75880 | tf_op jit(solution)/shard_map/while/body/eval_jaxpr/add | solution.py:90
  442.2 11.8 %gather_fusion = s32[2048]{0:T(1024)S(1)} fusion(s32[16384]{0:T(1024)S(1)} %get-tuple-element.674, s32[2048]{0:T(1024)S(1)} %broadcast_clamp_fusion.3), kind=kCustom, calls=%fused_computation.clone.clone.1 | custom fusion | bytes 24576 | tf_op jit(solution)/shard_map/while/body/eval_jaxpr/gather | solution.py:91
  458.6 8.8 %fusion.86 = (f32[2,1024]{1,0:T(2,128)S(1)}, f32[2048,2,1024]{2,0,1:T(8,128)}) fusion(pred[1024,2048]{0,1:T(8,128)(4,1)} %compare_and_fusion.2, bf16[1,2,1024,128]{3,2,1,0:T(8,128)(2,1)S(1)} %get-tuple-element.677, bf16[16384,128]{0,1:T(8,128)(2,1)} %get-tuple-element.676, s32[]{:T(128)S(6)} %select_n.474), kind=kOutput, calls=%fused_computation.5.clone.1 | convolution fusion | flops 1082128384 | bytes 19931140 | tf_op jit(solution)/shard_map/while/body/eval_jaxpr/kgqd,tkd->kgqt/dot_general | solution.py:35
  467.4 10.2 %fusion.89 = f32[1,2,1024,128]{3,2,1,0:T(8,128)} fusion(f32[2048,2,1024]{2,0,1:T(8,128)} %get-tuple-element.635, f32[2,1024]{1,0:T(2,128)S(1)} %bitcast.198, pred[1024,2048]{0,1:T(8,128)(4,1)} %compare_and_fusion.2, f32[1,2,1024,128]{3,2,1,0:T(8,128)} %get-tuple-element.656, bf16[16384,128]{1,0:T(8,128)(2,1)} %get-tuple-element.678, ...), kind=kOutput, calls=%fused_computation.12.clone.1 | convolution fusion | flops 1091305472 | bytes 21512196 | tf_op jit(solution)/shard_map/while/body/eval_jaxpr/kgqt,tkd->kgqd/dot_general | solution.py:42
  491.3 15.4 %fusion.85 = (s32[2048]{0:T(1024)S(1)}, s32[2048]{0:T(1024)S(1)}) fusion(s32[]{:T(128)S(6)} %mul.329, pred[2048]{0:T(1024)(128)(4,1)S(1)} %get-tuple-element.575, pred[2048]{0:T(1024)(128)(4,1)S(1)} %get-tuple-element.576, pred[2048]{0:T(1024)(128)(4,1)S(1)} %get-tuple-element.577, pred[2048]{0:T(1024)(128)(4,1)S(1)} %get-tuple-element.578, ...), kind=kLoop, calls=%fused_computation.66.clone.1 | loop fusion | flops 79872 | bytes 75880 | tf_op jit(solution)/shard_map/while/body/eval_jaxpr/add | solution.py:90
  506.8 11.8 %gather_fusion = s32[2048]{0:T(1024)S(1)} fusion(s32[16384]{0:T(1024)S(1)} %get-tuple-element.674, s32[2048]{0:T(1024)S(1)} %broadcast_clamp_fusion.3), kind=kCustom, calls=%fused_computation.clone.clone.1 | custom fusion | bytes 24576 | tf_op jit(solution)/shard_map/while/body/eval_jaxpr/gather | solution.py:91
  523.1 8.8 %fusion.86 = (f32[2,1024]{1,0:T(2,128)S(1)}, f32[2048,2,1024]{2,0,1:T(8,128)}) fusion(pred[1024,2048]{0,1:T(8,128)(4,1)} %compare_and_fusion.2, bf16[1,2,1024,128]{3,2,1,0:T(8,128)(2,1)S(1)} %get-tuple-element.677, bf16[16384,128]{0,1:T(8,128)(2,1)} %get-tuple-element.676, s32[]{:T(128)S(6)} %select_n.474), kind=kOutput, calls=%fused_computation.5.clone.1 | convolution fusion | flops 1082128384 | bytes 19931140 | tf_op jit(solution)/shard_map/while/body/eval_jaxpr/kgqd,tkd->kgqt/dot_general | solution.py:35
  532.0 10.2 %fusion.89 = f32[1,2,1024,128]{3,2,1,0:T(8,128)} fusion(f32[2048,2,1024]{2,0,1:T(8,128)} %get-tuple-element.635, f32[2,1024]{1,0:T(2,128)S(1)} %bitcast.198, pred[1024,2048]{0,1:T(8,128)(4,1)} %compare_and_fusion.2, f32[1,2,1024,128]{3,2,1,0:T(8,128)} %get-tuple-element.656, bf16[16384,128]{1,0:T(8,128)(2,1)} %get-tuple-element.678, ...), kind=kOutput, calls=%fused_computation.12.clone.1 | convolution fusion | flops 1091305472 | bytes 21512196 | tf_op jit(solution)/shard_map/while/body/eval_jaxpr/kgqt,tkd->kgqd/dot_general | solution.py:42
  555.9 15.4 %fusion.85 = (s32[2048]{0:T(1024)S(1)}, s32[2048]{0:T(1024)S(1)}) fusion(s32[]{:T(128)S(6)} %mul.329, pred[2048]{0:T(1024)(128)(4,1)S(1)} %get-tuple-element.575, pred[2048]{0:T(1024)(128)(4,1)S(1)} %get-tuple-element.576, pred[2048]{0:T(1024)(128)(4,1)S(1)} %get-tuple-element.577, pred[2048]{0:T(1024)(128)(4,1)S(1)} %get-tuple-element.578, ...), kind=kLoop, calls=%fused_computation.66.clone.1 | loop fusion | flops 79872 | bytes 75880 | tf_op jit(solution)/shard_map/while/body/eval_jaxpr/add | solution.py:90
  571.3 11.8 %gather_fusion = s32[2048]{0:T(1024)S(1)} fusion(s32[16384]{0:T(1024)S(1)} %get-tuple-element.674, s32[2048]{0:T(1024)S(1)} %broadcast_clamp_fusion.3), kind=kCustom, calls=%fused_computation.clone.clone.1 | custom fusion | bytes 24576 | tf_op jit(solution)/shard_map/while/body/eval_jaxpr/gather | solution.py:91
  587.7 8.8 %fusion.86 = (f32[2,1024]{1,0:T(2,128)S(1)}, f32[2048,2,1024]{2,0,1:T(8,128)}) fusion(pred[1024,2048]{0,1:T(8,128)(4,1)} %compare_and_fusion.2, bf16[1,2,1024,128]{3,2,1,0:T(8,128)(2,1)S(1)} %get-tuple-element.677, bf16[16384,128]{0,1:T(8,128)(2,1)} %get-tuple-element.676, s32[]{:T(128)S(6)} %select_n.474), kind=kOutput, calls=%fused_computation.5.clone.1 | convolution fusion | flops 1082128384 | bytes 19931140 | tf_op jit(solution)/shard_map/while/body/eval_jaxpr/kgqd,tkd->kgqt/dot_general | solution.py:35
  596.5 10.2 %fusion.89 = f32[1,2,1024,128]{3,2,1,0:T(8,128)} fusion(f32[2048,2,1024]{2,0,1:T(8,128)} %get-tuple-element.635, f32[2,1024]{1,0:T(2,128)S(1)} %bitcast.198, pred[1024,2048]{0,1:T(8,128)(4,1)} %compare_and_fusion.2, f32[1,2,1024,128]{3,2,1,0:T(8,128)} %get-tuple-element.656, bf16[16384,128]{1,0:T(8,128)(2,1)} %get-tuple-element.678, ...), kind=kOutput, calls=%fused_computation.12.clone.1 | convolution fusion | flops 1091305472 | bytes 21512196 | tf_op jit(solution)/shard_map/while/body/eval_jaxpr/kgqt,tkd->kgqd/dot_general | solution.py:42
  620.6 114.5 %reduce-scatter.2.cloned.1.call-done = bf16[1024,512]{1,0:T(8,128)(2,1)} async-done(((bf16[1024,4096]{1,0:T(8,128)(2,1)}), bf16[1024,512]{1,0:T(8,128)(2,1)}) %reduce-scatter.2.cloned.1.call-update) | async-done | bytes 1048592 | tf_op jit(solution)/shard_map/reduce_scatter | solution.py:99
  (274 shorter events, 227.4 us)
Async XLA Ops:
  6.5 608.4 %copy-start = (bf16[256,4096]{1,0:T(8,128)(2,1)S(1)}, bf16[256,4096]{1,0:T(8,128)(2,1)}, u32[]{:S(2)}) copy-start(bf16[256,4096]{1,0:T(8,128)(2,1)} %param.15) | copy-start | bytes 6291460
  6.5 11.2 %copy-start.5 = (bf16[4096,128]{1,0:T(8,128)(2,1)S(1)}, bf16[4096,128]{1,0:T(8,128)(2,1)}, u32[]{:S(2)}) copy-start(bf16[4096,128]{1,0:T(8,128)(2,1)} %param.14) | copy-start | bytes 3145732
  6.5 51.2 %all-gather.3.cloned.1.call-start = ((), (), s32[]{:S(2)}) async-start(), calls=%async_computation.1 | async-start | bytes 4456448 | tf_op jit(solution)/shard_map/all_gather | solution.py:76
  17.7 79.2 %all-gather.5.cloned.1.call-start = ((), (), s32[]{:S(2)}) async-start(), calls=%async_computation.2 | async-start | bytes 4456448 | tf_op jit(solution)/shard_map/all_gather | solution.py:77
  24.2 710.9 %reduce-scatter.2.cloned.1.call-start = ((), (), s32[]{:S(2)}) async-start(), calls=%async_computation.3 | async-start | bytes 9437184 | tf_op jit(solution)/shard_map/reduce_scatter | solution.py:99
  24.3 11.3 %copy-start.1 = (s32[16384]{0:T(1024)S(1)}, s32[16384]{0:T(1024)}, u32[]{:S(2)}) copy-start(s32[16384]{0:T(1024)} %param.10) | copy-start | bytes 196612
  31.8 65.1 %copy-start.4 = (s32[32]{0:T(128)S(1)}, s32[32]{0:T(128)}, u32[]{:S(2)}) copy-start(s32[32]{0:T(128)} %param.11) | copy-start | bytes 388
  144.9 11.7 %copy-start.2 = (f32[2048,2,1024]{2,0,1:T(8,128)S(1)}, f32[2048,2,1024]{2,0,1:T(8,128)}, u32[]{:S(2)}) copy-start(f32[2048,2,1024]{2,0,1:T(8,128)} %get-tuple-element.635) | copy-start | bytes 50331652 | tf_op jit(solution)/shard_map/while
  144.9 12.3 %copy-start.3 = (pred[1024,2048]{0,1:T(8,128)(4,1)S(1)}, pred[1024,2048]{0,1:T(8,128)(4,1)}, u32[]{:S(2)}) copy-start(pred[1024,2048]{0,1:T(8,128)(4,1)} %compare_and_fusion.2) | copy-start | bytes 6291460 | tf_op jit(solution)/shard_map/while
  209.2 12.0 %copy-start.2 = (f32[2048,2,1024]{2,0,1:T(8,128)S(1)}, f32[2048,2,1024]{2,0,1:T(8,128)}, u32[]{:S(2)}) copy-start(f32[2048,2,1024]{2,0,1:T(8,128)} %get-tuple-element.635) | copy-start | bytes 50331652 | tf_op jit(solution)/shard_map/while
  209.2 12.6 %copy-start.3 = (pred[1024,2048]{0,1:T(8,128)(4,1)S(1)}, pred[1024,2048]{0,1:T(8,128)(4,1)}, u32[]{:S(2)}) copy-start(pred[1024,2048]{0,1:T(8,128)(4,1)} %compare_and_fusion.2) | copy-start | bytes 6291460 | tf_op jit(solution)/shard_map/while
  273.7 12.0 %copy-start.2 = (f32[2048,2,1024]{2,0,1:T(8,128)S(1)}, f32[2048,2,1024]{2,0,1:T(8,128)}, u32[]{:S(2)}) copy-start(f32[2048,2,1024]{2,0,1:T(8,128)} %get-tuple-element.635) | copy-start | bytes 50331652 | tf_op jit(solution)/shard_map/while
  273.7 12.6 %copy-start.3 = (pred[1024,2048]{0,1:T(8,128)(4,1)S(1)}, pred[1024,2048]{0,1:T(8,128)(4,1)}, u32[]{:S(2)}) copy-start(pred[1024,2048]{0,1:T(8,128)(4,1)} %compare_and_fusion.2) | copy-start | bytes 6291460 | tf_op jit(solution)/shard_map/while
  338.3 12.0 %copy-start.2 = (f32[2048,2,1024]{2,0,1:T(8,128)S(1)}, f32[2048,2,1024]{2,0,1:T(8,128)}, u32[]{:S(2)}) copy-start(f32[2048,2,1024]{2,0,1:T(8,128)} %get-tuple-element.635) | copy-start | bytes 50331652 | tf_op jit(solution)/shard_map/while
  338.3 12.6 %copy-start.3 = (pred[1024,2048]{0,1:T(8,128)(4,1)S(1)}, pred[1024,2048]{0,1:T(8,128)(4,1)}, u32[]{:S(2)}) copy-start(pred[1024,2048]{0,1:T(8,128)(4,1)} %compare_and_fusion.2) | copy-start | bytes 6291460 | tf_op jit(solution)/shard_map/while
  402.8 12.0 %copy-start.2 = (f32[2048,2,1024]{2,0,1:T(8,128)S(1)}, f32[2048,2,1024]{2,0,1:T(8,128)}, u32[]{:S(2)}) copy-start(f32[2048,2,1024]{2,0,1:T(8,128)} %get-tuple-element.635) | copy-start | bytes 50331652 | tf_op jit(solution)/shard_map/while
  402.8 12.6 %copy-start.3 = (pred[1024,2048]{0,1:T(8,128)(4,1)S(1)}, pred[1024,2048]{0,1:T(8,128)(4,1)}, u32[]{:S(2)}) copy-start(pred[1024,2048]{0,1:T(8,128)(4,1)} %compare_and_fusion.2) | copy-start | bytes 6291460 | tf_op jit(solution)/shard_map/while
  467.4 12.0 %copy-start.2 = (f32[2048,2,1024]{2,0,1:T(8,128)S(1)}, f32[2048,2,1024]{2,0,1:T(8,128)}, u32[]{:S(2)}) copy-start(f32[2048,2,1024]{2,0,1:T(8,128)} %get-tuple-element.635) | copy-start | bytes 50331652 | tf_op jit(solution)/shard_map/while
  467.4 12.6 %copy-start.3 = (pred[1024,2048]{0,1:T(8,128)(4,1)S(1)}, pred[1024,2048]{0,1:T(8,128)(4,1)}, u32[]{:S(2)}) copy-start(pred[1024,2048]{0,1:T(8,128)(4,1)} %compare_and_fusion.2) | copy-start | bytes 6291460 | tf_op jit(solution)/shard_map/while
  531.9 12.0 %copy-start.2 = (f32[2048,2,1024]{2,0,1:T(8,128)S(1)}, f32[2048,2,1024]{2,0,1:T(8,128)}, u32[]{:S(2)}) copy-start(f32[2048,2,1024]{2,0,1:T(8,128)} %get-tuple-element.635) | copy-start | bytes 50331652 | tf_op jit(solution)/shard_map/while
  532.0 12.6 %copy-start.3 = (pred[1024,2048]{0,1:T(8,128)(4,1)S(1)}, pred[1024,2048]{0,1:T(8,128)(4,1)}, u32[]{:S(2)}) copy-start(pred[1024,2048]{0,1:T(8,128)(4,1)} %compare_and_fusion.2) | copy-start | bytes 6291460 | tf_op jit(solution)/shard_map/while
  596.5 12.0 %copy-start.2 = (f32[2048,2,1024]{2,0,1:T(8,128)S(1)}, f32[2048,2,1024]{2,0,1:T(8,128)}, u32[]{:S(2)}) copy-start(f32[2048,2,1024]{2,0,1:T(8,128)} %get-tuple-element.635) | copy-start | bytes 50331652 | tf_op jit(solution)/shard_map/while
  596.5 12.6 %copy-start.3 = (pred[1024,2048]{0,1:T(8,128)(4,1)S(1)}, pred[1024,2048]{0,1:T(8,128)(4,1)}, u32[]{:S(2)}) copy-start(pred[1024,2048]{0,1:T(8,128)(4,1)} %compare_and_fusion.2) | copy-start | bytes 6291460 | tf_op jit(solution)/shard_map/while
Sparse Core Ops, SparseCore 0:
  17.8 39.8 all-gather.2
  59.5 37.3 all-gather.4
  620.7 114.3 reduce-scatter.1
where the time goes:
time: 745 us; the launch traced here: 742 us
  other arithmetic  246 us (33%)
  matrix products  177 us (24%)
  waiting for transfers between devices  166 us (22%)
  local copies, waits for them, and re-layouts  138 us (19%)
  between operations  13.3 us (2%)
    add x8, other arithmetic, one_block(): span_order[global_rows // span_rows] * span_rows + global_rows % span_rows  123 us
    reduce_scatter x1, waiting for transfers between devices, per_device(): lax.psum_scatter(partial_value.astype(jnp.bfloat16), 'head', scatter_dime...  115 us
    gather x8, local copies, waits for them, and re-layouts, one_block(): key_seg = seg_ids[key_pos]  94.3 us
    dot_general x8, matrix products, update(): jnp.einsum('kgqt,tkd->kgqd', weights.astype(jnp.bfloat16), value_block, p...  81.7 us
    dot_general x8, matrix products, update(): jnp.einsum('kgqd,tkd->kgqt', query_part, key_block, preferred_element_typ...  70.1 us
    gather x112, other arithmetic, one_block(): span_order[global_rows // span_rows] * span_rows + global_rows % span_rows  47.9 us
    all_gather x1, waiting for transfers between devices, per_device(): value_piece = lax.all_gather(value_rows, 'ctx', axis=0, tiled=True)  39.1 us
    reduce_sum x8, other arithmetic, update(): totals = totals * factor + jnp.sum(weights, -1)  31.3 us
  transfers between devices with their start and end apart: 3, of which 3 were waited for; matrix products, arithmetic and copies ran while one was open for 4% of the time, Pallas kernels for 0%

commit v1 on v0

v1 whole, which is shorter than its diff:
```python
import functools
import math

import jax
import jax.numpy as jnp
import numpy as np
from jax import lax
from jax.experimental import pallas as pl
from jax.experimental.pallas import tpu as pltpu
from jax.sharding import PartitionSpec as P

HD = 128
SPAN = 512
SPANS = 32
CHUNKS = 4
rope_base = 500000.0
neg_large = -1e30
F32 = jnp.float32
BF16 = jnp.bfloat16
HBM = pl.BlockSpec(memory_space=pltpu.HBM)
ANYWHERE = pl.BlockSpec(memory_space=pl.ANY)
SCALAR = pl.BlockSpec(memory_space=pltpu.SMEM)
LOCAL = pl.BlockSpec(memory_space=pltpu.VMEM)
LIMIT = pltpu.CompilerParams(vmem_limit_bytes=20 * 2**20)
WIDE = pltpu.CompilerParams(vmem_limit_bytes=57 * 2**20)


def rope_tables():
    freq = rope_base ** (-np.arange(64, dtype=np.float64) * 2.0 / HD)
    sign = np.concatenate([-np.ones(64), np.ones(64)])

    def pair(pos):
        ang = np.concatenate([pos[:, None] * freq, pos[:, None] * freq], 1)
        return np.stack([np.cos(ang), np.sin(ang) * sign]).astype(np.float32)

    return pair(np.arange(SPANS) * float(SPAN)), pair(np.arange(SPAN) * 1.0)


def rotated(x, span, big_ref, small_ref):
    cb = big_ref[0, pl.ds(span, 1), :]
    sb = big_ref[1, pl.ds(span, 1), :]
    cs = small_ref[0]
    ss = small_ref[1]
    cos = cb * cs - sb * ss
    sin = sb * cs + cb * ss
    return x * cos + pltpu.roll(x, 64, 1) * sin


def own_spans(order_ref):
    me = lax.axis_index("ctx")
    a, b = order_ref[2 * me], order_ref[2 * me + 1]
    return jnp.where(a < b, 0, 1).astype(jnp.int32), jnp.minimum(a, b)


def bring(pairs_of_refs, sems, base):
    copies = [pltpu.make_async_copy(a, b, sems.at[base + t]) for t, (a, b) in enumerate(pairs_of_refs)]
    for copy in copies:
        copy.start()
    return copies


def project_kernel(
    order_ref, x_ref, wk_ref, wv_ref, wq_ref, big_ref, small_ref,
    kv_ref, q_ref, x_s, w_s, big_s, small_s, sems,
):
    slot, span = own_spans(order_ref)
    depth = x_s.shape[1] // CHUNKS
    copies = []
    for c in range(CHUNKS):
        part = pl.ds(c * depth, depth)
        copies.append(bring([
            (wk_ref.at[part, :], w_s.at[part, pl.ds(0, HD)]),
            (wv_ref.at[part, :], w_s.at[part, pl.ds(HD, HD)]),
            (wq_ref.at[part, :], w_s.at[part, pl.ds(2 * HD, 2 * HD)]),
            (x_ref.at[:, part], x_s.at[:, part]),
        ], sems, 4 * c))
    copies.append(bring([(big_ref, big_s), (small_ref, small_s)], sems, 4 * CHUNKS))
    y = jnp.zeros((2 * SPAN, 4 * HD), F32)
    for c in range(CHUNKS):
        for copy in copies[c]:
            copy.wait()
        part = slice(c * depth, (c + 1) * depth)
        y = y + jnp.dot(x_s[:, part], w_s[part, :], preferred_element_type=F32)
    for copy in copies[CHUNKS]:
        copy.wait()
    scale = HD ** (-0.5) * math.log2(math.e)

    for s in range(2):
        qs = s ^ slot
        here = jnp.where(qs == 0, span, SPANS - 1 - span)
        rows = slice(s * SPAN, (s + 1) * SPAN)
        to = pl.multiple_of(qs * 2 * SPAN, 2 * SPAN)
        kv_ref[pl.ds(to, SPAN), :] = rotated(y[rows, :HD], here, big_s, small_s).astype(BF16)
        for c in range(SPAN // HD):
            tile = y[s * SPAN + c * HD:s * SPAN + (c + 1) * HD, HD:2 * HD]
            kv_ref[pl.ds(to + SPAN + c * HD, HD), :] = tile.T.astype(BF16)
        for h in range(2):
            r = rotated(y[rows, (2 + h) * HD:(3 + h) * HD], here, big_s, small_s) * scale
            q_ref[qs, :, h * SPAN:(h + 1) * SPAN] = r.T.astype(BF16)


def project(order, states, w_key, w_value, w_query, tables):
    rows, width = states.shape
    return pl.pallas_call(
        project_kernel,
        in_specs=[SCALAR] + [HBM] * 6,
        out_specs=[LOCAL] * 2,
        out_shape=[
            jax.ShapeDtypeStruct((4 * SPAN, HD), BF16),
            jax.ShapeDtypeStruct((2, HD, 2 * SPAN), BF16),
        ],
        scratch_shapes=[
            pltpu.VMEM((rows, width), BF16),
            pltpu.VMEM((width, 4 * HD), BF16),
            *[pltpu.VMEM(t.shape, F32) for t in tables],
            pltpu.SemaphoreType.DMA((4 * CHUNKS + 2,)),
        ],
        compiler_params=WIDE,
        cost_estimate=pl.CostEstimate(flops=rows * width * 8 * HD, bytes_accessed=13 * 2**20, transcendentals=0),
    )(order, states, w_key, w_value, w_query, *tables)


def attn_kernel(many, units, asked, begins, ends, order_ref, start_ref, *refs):
    n = len(units)
    kv = refs[:many]
    q_ref = refs[many]
    at = many + 1
    before = {}
    for qs in asked:
        if qs not in begins:
            before[qs] = refs[at:at + 2]
            at += 2
    outs = {}
    for qs in asked:
        wide = 1 if qs in ends else 2
        outs[qs] = refs[at:at + wide]
        at += wide
    kb, vb, m_ref, acc_ref, span_ref, sems = refs[at:]
    me = lax.axis_index("ctx")
    x0, z0, c0 = me // 8, (me // 2) % 4, me % 2
    own = own_spans(order_ref)[1]

    for t, (src, base, where, late, _) in enumerate(units):
        pltpu.make_async_copy(kv[src].at[pl.ds(base, SPAN), :], kb.at[t], sems.at[t, 0]).start()
        for c in range(4):
            pltpu.make_async_copy(
                kv[src].at[pl.ds(base + SPAN + c * HD, HD), :],
                vb.at[t, pl.ds(0, HD), pl.ds(c * HD, HD)],
                sems.at[t, 1 + c],
            ).start()
        if isinstance(where, tuple):
            dx, dz, dc = where
            who = ((x0 ^ dx) * 4 + ((z0 + dz + 4) % 4)) * 2 + (c0 ^ dc)
        else:
            who = where
        early = jnp.minimum(order_ref[2 * who], order_ref[2 * who + 1])
        span = SPANS - 1 - early if late else early
        if not isinstance(where, tuple):
            span = jnp.where(me == who, SPANS, span)
        span_ref[t] = span
    vb[:, HD:, :] = jnp.ones((n, 16, SPAN), BF16)
    for qs in asked:
        if qs in begins:
            m_ref[qs] = jnp.full(m_ref.shape[1:], neg_large, F32)
            acc_ref[qs] = jnp.zeros(acc_ref.shape[1:], F32)
        else:
            m_ref[qs] = before[qs][0][...]
            acc_ref[qs] = before[qs][1][...]

    def first_of(p):
        low = jnp.int32(0)
        for d in range(3):
            s = start_ref[d]
            low = jnp.where(s <= p, s, low)
        return low

    def block(u, qs, masked):
        k = kb[u]
        v = vb[u]
        qspan = SPANS - 1 - own if qs else own
        wide = 256
        parts = [slice(c * wide, (c + 1) * wide) for c in range(2 * SPAN // wide)]
        scores = [jnp.dot(k, q_ref[qs, :, sl], preferred_element_type=F32) for sl in parts]
        weights, factors = [], []
        for s, sl in zip(scores, parts):
            if masked:
                qpos = lax.broadcasted_iota(jnp.int32, (1, wide), 1) + (sl.start % SPAN + qspan * SPAN)
                low = first_of(qpos)
                kpos = lax.broadcasted_iota(jnp.int32, (SPAN, 1), 0) + span_ref[u] * SPAN
                s = jnp.where((kpos <= qpos) & (kpos >= low), s, neg_large)
            old = m_ref[qs, :, sl]
            new = jnp.maximum(old, jnp.max(s, 0, keepdims=True))
            weights.append(jnp.exp2(s - new).astype(BF16))
            factors.append(jnp.exp2(old - new))
            m_ref[qs, :, sl] = new
        for p, f, sl in zip(weights, factors, parts):
            acc_ref[qs, :, sl] = acc_ref[qs, :, sl] * f + jnp.dot(v, p, preferred_element_type=F32)

    def visit(u, qs):
        qspan = SPANS - 1 - own if qs else own
        kspan = span_ref[u]
        low_first = first_of(qspan * SPAN)
        low_last = first_of(qspan * SPAN + SPAN - 1)
        seen = (kspan <= qspan) & (kspan * SPAN + SPAN - 1 >= low_first)
        cut = (kspan == qspan) | (kspan * SPAN < low_last)

        @pl.when(seen & cut)
        def _():
            block(u, qs, True)

        @pl.when(seen & jnp.logical_not(cut))
        def _():
            block(u, qs, False)

    def steps(first, last, who):
        def step(u, carry):
            pltpu.make_async_copy(kb.at[u], kb.at[u], sems.at[u, 0]).wait()
            for c in range(4):
                spot = vb.at[u, pl.ds(0, HD), pl.ds(c * HD, HD)]
                pltpu.make_async_copy(spot, spot, sems.at[u, 1 + c]).wait()
            for qs in who:
                visit(u, qs)
            return carry

        lax.fori_loop(first, last, step, 0)

    t = 0
    while t < n:
        e = t
        while e < n and units[e][4] == units[t][4]:
            e += 1
        steps(t, e, units[t][4])
        t = e

    for qs in asked:
        if qs in ends:
            for h in range(2):
                sl = slice(h * SPAN, (h + 1) * SPAN)
                value = acc_ref[qs, 0:HD, sl] / acc_ref[qs, HD:HD + 1, sl]
                outs[qs][0][:, h * HD:(h + 1) * HD] = value.T.astype(BF16)
        else:
            outs[qs][0][...] = m_ref[qs]
            outs[qs][1][...] = acc_ref[qs]


def attend(order, starts, arrays, units, q, states, ends=()):
    n = len(units)
    many = len(arrays)
    asked = tuple(sorted(states))
    begins = tuple(s for s in asked if states[s] is None)
    inner = []
    shapes = []
    for s in asked:
        if s not in begins:
            inner += list(states[s])
        if s in ends:
            shapes.append(jax.ShapeDtypeStruct((SPAN, 2 * HD), BF16))
        else:
            shapes.append(jax.ShapeDtypeStruct((1, 2 * SPAN), F32))
            shapes.append(jax.ShapeDtypeStruct((HD + 16, 2 * SPAN), F32))
    work = sum(len(u[4]) for u in units)
    got = pl.pallas_call(
        functools.partial(attn_kernel, many, units, asked, begins, ends),
        in_specs=[SCALAR, SCALAR] + [ANYWHERE] * many + [LOCAL] * (1 + len(inner)),
        out_specs=[LOCAL] * len(shapes),
        out_shape=shapes,
        scratch_shapes=[
            pltpu.VMEM((n, SPAN, HD), BF16),
            pltpu.VMEM((n, HD + 16, SPAN), BF16),
            pltpu.VMEM((2, 1, 2 * SPAN), F32),
            pltpu.VMEM((2, HD + 16, 2 * SPAN), F32),
            pltpu.SMEM((n,), jnp.int32),
            pltpu.SemaphoreType.DMA((n, 5)),
        ],
        compiler_params=LIMIT,
        cost_estimate=pl.CostEstimate(
            flops=work * 10**6, bytes_accessed=n * 2**10, transcendentals=work * 2**10
        ),
    )(order, starts, *arrays, q, *inner)
    out = {}
    at = 0
    for s in asked:
        if s in ends:
            out[s] = got[at]
            at += 1
        else:
            out[s] = (got[at], got[at + 1])
            at += 2
    return out


def out_kernel(first, *refs):
    parts, w_ref, straight, crossed, out_ref, w_s, sems = refs[0:4], refs[4], refs[5:8], refs[8:11], *refs[11:]
    head = lax.axis_index("head").astype(jnp.int32)
    core = lax.axis_index("ctx") % 2
    cols = out_ref.shape[1]
    block = head + 1 - 2 * (head % 2) if first else head
    at = pl.multiple_of(block * cols, cols)
    own = pltpu.make_async_copy(w_ref.at[:, pl.ds(at, cols)], w_s.at[0], sems.at[0])
    own.start()

    def fetch(source):
        for t in range(3):
            pltpu.make_async_copy(source[t], w_s.at[1 + t], sems.at[1 + t]).start()

    use_straight = core == (1 if first else 0)

    @pl.when(use_straight)
    def _():
        fetch(straight)

    @pl.when(jnp.logical_not(use_straight))
    def _():
        fetch(crossed)

    total = None
    for t in range(4):
        pltpu.make_async_copy(w_s.at[t], w_s.at[t], sems.at[t]).wait()
        part = jnp.dot(parts[t][...], w_s[t], preferred_element_type=F32)
        total = part if total is None else total + part
    out_ref[...] = total.astype(out_ref.dtype)


def output(parts, straight, crossed, w_out, first):
    cols = w_out.shape[1] // 8
    return pl.pallas_call(
        functools.partial(out_kernel, first),
        in_specs=[LOCAL] * 4 + [ANYWHERE] * 7,
        out_specs=LOCAL,
        out_shape=jax.ShapeDtypeStruct((SPAN, cols), BF16 if first else F32),
        scratch_shapes=[pltpu.VMEM((4, 2 * HD, cols), BF16), pltpu.SemaphoreType.DMA((4,))],
        compiler_params=LIMIT,
        cost_estimate=pl.CostEstimate(flops=SPAN * 1024 * cols * 2, bytes_accessed=3 * 2**20, transcendentals=0),
    )(*parts, w_out, *straight, *crossed)


def join_kernel(order_ref, own0, other0, own1, other1, out_ref):
    slot = own_spans(order_ref)[0]
    for qs, (own, other) in enumerate(((own0, other0), (own1, other1))):
        row = pl.multiple_of((slot ^ qs) * SPAN, SPAN)
        out_ref[pl.ds(row, SPAN), :] = (own[...] + other[...].astype(F32)).astype(BF16)


def join(order, own, other):
    cols = own[0].shape[1]
    return pl.pallas_call(
        join_kernel,
        in_specs=[SCALAR] + [LOCAL] * 4,
        out_specs=LOCAL,
        out_shape=jax.ShapeDtypeStruct((2 * SPAN, cols), BF16),
        compiler_params=LIMIT,
        cost_estimate=pl.CostEstimate(flops=2 * SPAN * cols, bytes_accessed=4 * 2**20, transcendentals=0),
    )(order, own[0], other[0], own[1], other[1])


def pairs(move):
    def flat(x, y, z, c):
        x, y, z, c = x % 4, y % 4, z % 4, c % 2
        return ((x % 2 * 4 + z) * 2 + c) * 8 + y * 2 + x // 2

    return [
        (flat(x, y, z, c), flat(*move(x, y, z, c)))
        for x in range(4) for y in range(4) for z in range(4) for c in range(2)
    ]


to_pair = pairs(lambda x, y, z, c: (x ^ 1, y, z, c))
to_far = pairs(lambda x, y, z, c: (x + 2, y, z, c))
to_core = pairs(lambda x, y, z, c: (x, y, z, c + 1))
z_up = pairs(lambda x, y, z, c: (x, y, z + 1, c))
z_down = pairs(lambda x, y, z, c: (x, y, z - 1, c))
y_up = pairs(lambda x, y, z, c: (x, y + 1, z, c))
y_down = pairs(lambda x, y, z, c: (x, y - 1, z, c))
y_two = pairs(lambda x, y, z, c: (x, y + 2, z, c))


def send(value, to):
    return lax.ppermute(value, ("ctx", "head"), to)


def after(values, *others):
    return lax.optimization_barrier((values, others))[0]


def per_device(states, seg_ids, span_order, w_query, w_key, w_value, w_out):
    head = lax.axis_index("head").astype(jnp.int32)
    core = lax.axis_index("ctx").astype(jnp.int32) % 2
    y, far = head // 2, head % 2
    starts = jnp.sum(seg_ids[None, :] < jnp.arange(1, 4, dtype=jnp.int32)[:, None], 1, dtype=jnp.int32)
    tables = tuple(jnp.asarray(t) for t in rope_tables())

    rels = {
        "own": (0, 0), "pair": (1, 0), "below": (0, -1), "above": (0, 1),
        "pair_below": (1, -1), "pair_above": (1, 1), "two": (0, 2), "far": (1, 2),
    }
    held = {}

    def hold(name, crossed, array):
        for late in (0, 1):
            held[name, late, crossed] = (array, late * 2 * SPAN)

    def across_cores(names, *others):
        values = tuple(held[name, 0, 0][0] for name in names)
        for name, value in zip(names, after(values, *others) if others else values):
            hold(name, 1, send(value, to_core))

    def stage(picks, state, ends=()):
        arrays, units, index = [], [], {}
        for names, late, who in picks:
            for name in names:
                for c in (0, 1):
                    array, row = held[name, late, c]
                    if id(array) not in index:
                        index[id(array)] = len(arrays)
                        arrays.append(array)
                    units.append((index[id(array)], row, (*rels[name], c), late, who))
        return attend(span_order, starts, arrays, tuple(units), q, state, ends)

    own, q = project(span_order, states, w_key, w_value, w_query, tables)
    hold("own", 0, own)
    below, above, pair = send(own, z_up), send(own, z_down), send(own, to_pair)
    across_cores(("own",))

    half = w_out.shape[1] // 8

    def columns(step):
        block = 2 * ((y + step) % 4) + (far ^ core)
        return lax.dynamic_slice_in_dim(w_out, block * half, half, 1)

    straight = [send(columns(1), y_up), send(columns(3), y_down), send(columns(2), y_two)]
    both, ql, qe = (0, 1), (1,), (0,)
    s = stage([(("own",), 0, both), (("own",), 1, ql)], {0: None, 1: None})
    below, pair, above, straight = after((below, pair, above, straight), s)
    hold("below", 0, below)
    hold("above", 0, above)
    hold("pair", 0, pair)
    two = send(below, z_up)
    pair_above = send(pair, z_down)
    pair_below = send(below, to_pair)
    near = ("below", "above", "pair")
    across_cores(near)
    crossed = [send(w, to_core) for w in straight]
    s = stage([(near, 0, both), (near, 1, ql)], s)
    two, pair_above, pair_below = after((two, pair_above, pair_below), s)
    hold("two", 0, two)
    hold("pair_above", 0, pair_above)
    hold("pair_below", 0, pair_below)
    far_early = send(pair_below[:2 * SPAN], z_up)
    far_late = send(pair_above[2 * SPAN:], z_down)
    rest = ("two", "pair_above", "pair_below")
    across_cores(rest)
    s = stage([(rest, 0, both)], s)
    far_early = after(far_early, s)
    held["far", 0, 0] = (far_early, 0)
    held["far", 0, 1] = (send(far_early, to_core), 0)
    early = stage([(("far",), 0, qe)], {0: s[0]}, qe)[0]
    early_up, early_down = send(early, y_up), send(early, y_down)
    s = stage([(("far",), 0, ql), (rest, 1, ql)], {1: after(s[1], early)})
    far_late, early_up = after((far_late, early_up), s)
    early_across = send(early_up, y_up)
    held["far", 1, 0] = (far_late, 0)
    held["far", 1, 1] = (send(far_late, to_core), 0)
    late = stage([(("far",), 1, ql)], s, ql)[1]
    late_up, late_down = send(late, y_up), send(late, y_down)

    early_parts = [early, early_up, early_down, early_across]
    early_theirs = output(after(early_parts, late), straight, crossed, w_out, True)
    early_other = send(early_theirs, to_far)
    late_up, late_down = after((late_up, late_down), early_theirs)
    late_parts = [late, late_up, late_down, send(late_down, y_down)]
    late_theirs = output(late_parts, straight, crossed, w_out, True)
    late_other = send(late_theirs, to_far)
    early_own = output(after(early_parts, early_theirs), straight, crossed, w_out, False)
    late_own = output(after(late_parts, late_theirs), straight, crossed, w_out, False)
    return join(span_order, [early_own, late_own], [early_other, late_other])


def solution(mesh):
    in_specs = (
        P("ctx", None),
        P(),
        P(),
        P(None, "head"),
        P(None, "head"),
        P(None, "head"),
        P("head", None),
    )
    out_specs = P("ctx", "head")
    return jax.shard_map(
        per_device, mesh=mesh, in_specs=in_specs, out_specs=out_specs, check_vma=False
    )
```

time: 745 us -> 125 us (0.17)
  other arithmetic: 246 us -> 0.32 us
  matrix products: 177 us -> 0 us
  local copies, waits for them, and re-layouts: 138 us -> 0.13 us
  waiting for transfers between devices: 166 us -> 51.4 us
  Pallas kernels: 0 us -> 37.6 us
  starting transfers between devices: 0.09 us -> 35 us
  between operations: 13.3 us -> 0.31 us
    dot_general x20 -> x0, matrix products: 177 us -> none  [the longest x8 81.7 us: update(): jnp.einsum('kgqt,tkd->kgqd', weights.astype(jnp.bfloat16), value_block, p...]
    add x24 -> x1, other arithmetic: 123 us -> 0.01 us  [per_device(): jnp.arange(1, 4, dtype=jnp.int32)[:, None]]
    reduce_scatter x1 -> x0, waiting for transfers between devices: 115 us -> none  [per_device(): lax.psum_scatter(partial_value.astype(jnp.bfloat16), 'head', scatter_dime...]
    gather x26 -> x0, local copies, waits for them, and re-layouts: 112 us -> none  [the longest x8 94.3 us: one_block(): key_seg = seg_ids[key_pos]]
    ppermute x0 -> x31, waiting for transfers between devices: none -> 51.4 us  [send(): return lax.ppermute(value, ('ctx', 'head'), to)]
    all_gather x2 -> x0, waiting for transfers between devices: 51.3 us -> none  [the longest x1 39.1 us: per_device(): value_piece = lax.all_gather(value_rows, 'ctx', axis=0, tiled=True)]
    gather x121 -> x0, other arithmetic: 48 us -> none  [the longest x112 47.9 us: one_block(): span_order[global_rows // span_rows] * span_rows + global_rows % span_rows]
    pallas_call x0 -> x12, Pallas kernels: none -> 37.6 us  [the longest x6 21.9 us: attend(): pl.pallas_call(functools.partial(attn_kernel, many, units, asked, begins,...]
  transfers between devices with their start and end apart: 3 -> 31, of which waited for: 3 -> 18; matrix products, arithmetic and copies ran while one was open for 4% -> 0% of each run, Pallas kernels for 0% -> 21%
where the time goes in v1:
time: 125 us
  waiting for transfers between devices  51.4 us (41%)
  Pallas kernels  37.6 us (30%)
  starting transfers between devices  35 us (28%)
    ppermute x31, waiting for transfers between devices, send(): return lax.ppermute(value, ('ctx', 'head'), to)  51.4 us
    ppermute x31, starting transfers between devices, send(): return lax.ppermute(value, ('ctx', 'head'), to)  35 us
    pallas_call x6, Pallas kernels, attend(): pl.pallas_call(functools.partial(attn_kernel, many, units, asked, begins,...  21.9 us
    pallas_call x1, Pallas kernels, project(): pl.pallas_call(project_kernel, in_specs=[SCALAR] + [HBM] * 6, out_specs=[...  10.2 us
    pallas_call x4, Pallas kernels, output(): pl.pallas_call(functools.partial(out_kernel, first), in_specs=[LOCAL] * 4...  3.83 us
  transfers between devices with their start and end apart: 31, of which 18 were waited for; matrix products, arithmetic and copies ran while one was open for 0% of the time, Pallas kernels for 21%

profile of v1, /device:TPU:0, one launch (start us, length us, event | category | flops | bytes accessed | tf_op | source)
XLA Modules:
  0.0 124.8 jit_solution(15972008626359484249)
XLA Ops:
  0.0 10.2 %shard_map.91 = (bf16[2048,128]{1,0:T(8,128)(2,1)}, bf16[2,128,1024]{2,1,0:T(8,128)(2,1)}) custom-call(s32[32]{0:T(128)} %order_ref.15, bf16[1024,4096]{1,0:T(8,128)(2,1)} %x_ref.1, bf16[4096,128]{1,0:T(8,128)(2,1)} %wk_ref.1, bf16[4096,128]{1,0:T(8,128)(2,1)} %wv_ref.1, bf16[4096,256]{1,0:T(8,128)(2,1)} %wq_ref.1, f32[2,32,128]{2,1,0:T(8,128)} %constant.67.clone.big_ref, ...), custom_call_target="tpu_custom_call" | custom-call | flops 4294967296 | bytes 13631488 | tf_op jit(solution)/shard_map/pallas_call | solution.py:104
  10.5 1.7 %collective-permute-start.3 = (bf16[256,512]{1,0:T(8,128)(2,1)S(1)}, bf16[256,512]{1,0:T(8,128)(2,1)S(1)}, u32[]{:S(2)}, u32[]{:S(2)}) collective-permute-start(bf16[256,512]{1,0:T(8,128)(2,1)S(1)} %get-tuple-element.95), channel_id=1, source_target_pairs={{0,2},{8,10},{16,18},{24,26},{32,34},{40,42},{48,50},{56,58},{2,4}... | collective-permute-start | bytes 786440 | tf_op jit(solution)/shard_map/ppermute | solution.py:378
  12.2 1.9 %collective-permute-start = (bf16[2048,128]{1,0:T(8,128)(2,1)}, bf16[2048,128]{1,0:T(8,128)(2,1)S(1)}, u32[]{:S(2)}, u32[]{:S(2)}) collective-permute-start(bf16[2048,128]{1,0:T(8,128)(2,1)} %get-tuple-element.49.refs_0_), channel_id=1, source_target_pairs={{0,16},{8,24},{16,32},{24,40},{32,48},{40,56},{48,0},{56,8},{2,18}... | collective-permute-start | bytes 1572872 | tf_op jit(solution)/shard_map/ppermute | solution.py:378
  15.7 2.1 %collective-permute-start.2 = (bf16[2048,128]{1,0:T(8,128)(2,1)}, bf16[2048,128]{1,0:T(8,128)(2,1)S(1)}, u32[]{:S(2)}, u32[]{:S(2)}) collective-permute-start(bf16[2048,128]{1,0:T(8,128)(2,1)} %get-tuple-element.49.refs_0_), channel_id=1, source_target_pairs={{0,48},{8,56},{16,0},{24,8},{32,16},{40,24},{48,32},{56,40},{2,50}... | collective-permute-start | bytes 1572872 | tf_op jit(solution)/shard_map/ppermute | solution.py:378
  17.8 2.7 %collective-permute-done.3.refs_5_ = bf16[256,512]{1,0:T(8,128)(2,1)S(1)} collective-permute-done((bf16[256,512]{1,0:T(8,128)(2,1)S(1)}, bf16[256,512]{1,0:T(8,128)(2,1)S(1)}, u32[]{:S(2)}, u32[]{:S(2)}) %collective-permute-start.3) | collective-permute-done | bytes 262176 | tf_op jit(solution)/shard_map/ppermute | solution.py:378
  20.5 1.7 %collective-permute-start.4 = (bf16[256,512]{1,0:T(8,128)(2,1)S(1)}, bf16[256,512]{1,0:T(8,128)(2,1)S(1)}, u32[]{:S(2)}, u32[]{:S(2)}) collective-permute-start(bf16[256,512]{1,0:T(8,128)(2,1)S(1)} %get-tuple-element.94), channel_id=1, source_target_pairs={{0,6},{8,14},{16,22},{24,30},{32,38},{40,46},{48,54},{56,62},{2,0}... | collective-permute-start | bytes 786440 | tf_op jit(solution)/shard_map/ppermute | solution.py:378
  23.2 4.8 %shard_map.92 = (f32[1,1024]{1,0:T(1,128)S(1)}, f32[144,1024]{1,0:T(8,128)S(1)}, f32[1,1024]{1,0:T(1,128)S(1)}, f32[144,1024]{1,0:T(8,128)S(1)}) custom-call(s32[32]{0:T(128)S(1)} %copy-done.3, s32[3]{0:T(128)S(1)} %convert_reduce_fusion.start_ref, bf16[2048,128]{1,0:T(8,128)(2,1)S(1)} %copy-done.2, bf16[2048,128]{1,0:T(8,128)(2,1)} %collective-permute-done.6.refs_1_, ...), custom_call_target="tpu_custom_call" | custom-call | flops 6000000 | bytes 4096 | tf_op jit(solution)/shard_map/pallas_call | solution.py:262
  28.0 1.7 %collective-permute-done.4.refs_6_ = bf16[256,512]{1,0:T(8,128)(2,1)S(1)} collective-permute-done((bf16[256,512]{1,0:T(8,128)(2,1)S(1)}, bf16[256,512]{1,0:T(8,128)(2,1)S(1)}, u32[]{:S(2)}, u32[]{:S(2)}) %collective-permute-start.4) | collective-permute-done | bytes 262176 | tf_op jit(solution)/shard_map/ppermute | solution.py:378
  29.7 1.5 %collective-permute-done.5.refs_7_ = bf16[256,512]{1,0:T(8,128)(2,1)S(1)} collective-permute-done((bf16[256,512]{1,0:T(8,128)(2,1)S(1)}, bf16[256,512]{1,0:T(8,128)(2,1)S(1)}, u32[]{:S(2)}, u32[]{:S(2)}) %collective-permute-start.5) | collective-permute-done | bytes 262176 | tf_op jit(solution)/shard_map/ppermute | solution.py:378
  32.0 1.9 %collective-permute-start.7 = (bf16[2048,128]{1,0:T(8,128)(2,1)S(1)}, bf16[2048,128]{1,0:T(8,128)(2,1)S(1)}, u32[]{:S(2)}, u32[]{:S(2)}) collective-permute-start(bf16[2048,128]{1,0:T(8,128)(2,1)S(1)} %collective-permute-done.refs_0_), channel_id=1, source_target_pairs={{0,16},{8,24},{16,32},{24,40},{32,48},{40,56},{48,0},{56,8},{2,18}... | collective-permute-start | bytes 1572872 | tf_op jit(solution)/shard_map/ppermute | solution.py:378
  33.9 2.1 %collective-permute-start.8 = (bf16[2048,128]{1,0:T(8,128)(2,1)S(1)}, bf16[2048,128]{1,0:T(8,128)(2,1)S(1)}, u32[]{:S(2)}, u32[]{:S(2)}) collective-permute-start(bf16[2048,128]{1,0:T(8,128)(2,1)S(1)} %collective-permute-done.1.refs_4_), channel_id=1, source_target_pairs={{0,48},{8,56},{16,0},{24,8},{32,16},{40,24},{48,32},{56,40},{2,50}... | collective-permute-start | bytes 1572872 | tf_op jit(solution)/shard_map/ppermute | solution.py:378
  36.0 1.5 %collective-permute-start.9 = (bf16[2048,128]{1,0:T(8,128)(2,1)S(1)}, bf16[2048,128]{1,0:T(8,128)(2,1)S(1)}, u32[]{:S(2)}, u32[]{:S(2)}) collective-permute-start(bf16[2048,128]{1,0:T(8,128)(2,1)S(1)} %collective-permute-done.refs_0_), channel_id=1, source_target_pairs={{0,64},{8,72},{16,80},{24,88},{32,96},{40,104},{48,112},{56,120},{... | collective-permute-start | bytes 1572872 | tf_op jit(solution)/shard_map/ppermute | solution.py:378
  37.5 6.7 %shard_map.93 = (f32[1,1024]{1,0:T(1,128)S(1)}, f32[144,1024]{1,0:T(8,128)S(1)}, f32[1,1024]{1,0:T(1,128)S(1)}, f32[144,1024]{1,0:T(8,128)S(1)}) custom-call(s32[32]{0:T(128)S(1)} %copy-done.3, s32[3]{0:T(128)S(1)} %convert_reduce_fusion.start_ref, bf16[2048,128]{1,0:T(8,128)(2,1)S(1)} %collective-permute-done.refs_0_, ...), custom_call_target="tpu_custom_call" | custom-call | flops 18000000 | bytes 12288 | tf_op jit(solution)/shard_map/pallas_call | solution.py:262
  44.2 4.3 %collective-permute-done.7.refs_0_.refs_2_ = bf16[2048,128]{1,0:T(8,128)(2,1)S(1)} collective-permute-done((bf16[2048,128]{1,0:T(8,128)(2,1)S(1)}, bf16[2048,128]{1,0:T(8,128)(2,1)S(1)}, u32[]{:S(2)}, u32[]{:S(2)}) %collective-permute-start.7) | collective-permute-done | bytes 524320 | tf_op jit(solution)/shard_map/ppermute | solution.py:378
  48.5 1.5 %collective-permute-done.9.refs_4_.refs_6_ = bf16[2048,128]{1,0:T(8,128)(2,1)S(1)} collective-permute-done((bf16[2048,128]{1,0:T(8,128)(2,1)S(1)}, bf16[2048,128]{1,0:T(8,128)(2,1)S(1)}, u32[]{:S(2)}, u32[]{:S(2)}) %collective-permute-start.9) | collective-permute-done | bytes 524320 | tf_op jit(solution)/shard_map/ppermute | solution.py:378
  53.8 4.2 %shard_map.94 = (f32[1,1024]{1,0:T(1,128)S(1)}, f32[144,1024]{1,0:T(8,128)S(1)}, f32[1,1024]{1,0:T(1,128)S(1)}, f32[144,1024]{1,0:T(8,128)S(1)}) custom-call(s32[32]{0:T(128)S(1)} %copy-done.3, s32[3]{0:T(128)S(1)} %convert_reduce_fusion.start_ref, bf16[2048,128]{1,0:T(8,128)(2,1)S(1)} %collective-permute-done.7.refs_0_.refs_2_, ...), custom_call_target="tpu_custom_call" | custom-call | flops 12000000 | bytes 6144 | tf_op jit(solution)/shard_map/pallas_call | solution.py:262
  57.9 2.9 %collective-permute-done.13.refs_0_ = bf16[1024,128]{1,0:T(8,128)(2,1)S(1)} collective-permute-done((bf16[1024,128]{1,0:T(8,128)(2,1)S(1)}, bf16[1024,128]{1,0:T(8,128)(2,1)S(1)}, u32[]{:S(2)}, u32[]{:S(2)}) %collective-permute-start.13) | collective-permute-done | bytes 262176 | tf_op jit(solution)/shard_map/ppermute | solution.py:378
  60.9 1.7 %collective-permute-start.17 = (bf16[1024,128]{1,0:T(8,128)(2,1)S(1)}, bf16[1024,128]{1,0:T(8,128)(2,1)S(1)}, u32[]{:S(2)}, u32[]{:S(2)}) collective-permute-start(bf16[1024,128]{1,0:T(8,128)(2,1)S(1)} %collective-permute-done.13.refs_0_), channel_id=1, source_target_pairs={{0,8},{8,0},{16,24},{24,16},{32,40},{40,32},{48,56},{56,48},{2,10}... | collective-permute-start | bytes 786440 | tf_op jit(solution)/shard_map/ppermute | solution.py:378
  65.0 4.1 %collective-permute-start.19 = (bf16[512,256]{1,0:T(8,128)(2,1)S(1)}, bf16[512,256]{1,0:T(8,128)(2,1)S(1)}, u32[]{:S(2)}, u32[]{:S(2)}) collective-permute-start(bf16[512,256]{1,0:T(8,128)(2,1)S(1)} %shard_map.95.refs_0_), channel_id=1, source_target_pairs={{0,2},{8,10},{16,18},{24,26},{32,34},{40,42},{48,50},{56,58},{2,4}... | collective-permute-start | bytes 786440 | tf_op jit(solution)/shard_map/ppermute | solution.py:378
  69.0 3.7 %shard_map.96 = (f32[1,1024]{1,0:T(1,128)S(1)}, f32[144,1024]{1,0:T(8,128)S(1)}) custom-call(s32[32]{0:T(128)S(1)} %copy-done.3, s32[3]{0:T(128)S(1)} %convert_reduce_fusion.start_ref, bf16[1024,128]{1,0:T(8,128)(2,1)S(1)} %collective-permute-done.13.refs_0_, bf16[1024,128]{1,0:T(8,128)(2,1)S(1)} %collective-permute-done.17.refs_1_, ...), custom_call_target="tpu_custom_call" | custom-call | flops 8000000 | bytes 8192 | tf_op jit(solution)/shard_map/pallas_call | solution.py:262
  72.8 4.7 %collective-permute-done.19.refs_1_ = bf16[512,256]{1,0:T(8,128)(2,1)S(1)} collective-permute-done((bf16[512,256]{1,0:T(8,128)(2,1)S(1)}, bf16[512,256]{1,0:T(8,128)(2,1)S(1)}, u32[]{:S(2)}, u32[]{:S(2)}) %collective-permute-start.19) | collective-permute-done | bytes 262176 | tf_op jit(solution)/shard_map/ppermute | solution.py:378
  77.6 1.9 %collective-permute-start.20 = (bf16[512,256]{1,0:T(8,128)(2,1)S(1)}, bf16[512,256]{1,0:T(8,128)(2,1)S(1)}, u32[]{:S(2)}, u32[]{:S(2)}) collective-permute-start(bf16[512,256]{1,0:T(8,128)(2,1)S(1)} %shard_map.95.refs_0_), channel_id=1, source_target_pairs={{0,6},{8,14},{16,22},{24,30},{32,38},{40,46},{48,54},{56,62},{2,0}... | collective-permute-start | bytes 786440 | tf_op jit(solution)/shard_map/ppermute | solution.py:378
  81.4 4.8 %collective-permute-done.20.refs_2_ = bf16[512,256]{1,0:T(8,128)(2,1)S(1)} collective-permute-done((bf16[512,256]{1,0:T(8,128)(2,1)S(1)}, bf16[512,256]{1,0:T(8,128)(2,1)S(1)}, u32[]{:S(2)}, u32[]{:S(2)}) %collective-permute-start.20) | collective-permute-done | bytes 262176 | tf_op jit(solution)/shard_map/ppermute | solution.py:378
  87.2 1.7 %collective-permute-done.21.refs_3_ = bf16[512,256]{1,0:T(8,128)(2,1)S(1)} collective-permute-done((bf16[512,256]{1,0:T(8,128)(2,1)S(1)}, bf16[512,256]{1,0:T(8,128)(2,1)S(1)}, u32[]{:S(2)}, u32[]{:S(2)}) %collective-permute-start.21) | collective-permute-done | bytes 262176 | tf_op jit(solution)/shard_map/ppermute | solution.py:378
  90.5 4.9 %collective-permute-done.27.refs_1_ = bf16[512,256]{1,0:T(8,128)(2,1)S(1)} collective-permute-done((bf16[512,256]{1,0:T(8,128)(2,1)S(1)}, bf16[512,256]{1,0:T(8,128)(2,1)S(1)}, u32[]{:S(2)}, u32[]{:S(2)}) %collective-permute-start.27) | collective-permute-done | bytes 262176 | tf_op jit(solution)/shard_map/ppermute | solution.py:378
  96.2 2.0 %collective-permute-start.29 = (bf16[512,256]{1,0:T(8,128)(2,1)S(1)}, bf16[512,256]{1,0:T(8,128)(2,1)S(1)}, u32[]{:S(2)}, u32[]{:S(2)}) collective-permute-start(bf16[512,256]{1,0:T(8,128)(2,1)S(1)} %collective-permute-done.28.refs_2_), channel_id=1, source_target_pairs={{0,6},{8,14},{16,22},{24,30},{32,38},{40,46},{48,54},{56,62},{2,0}... | collective-permute-start | bytes 786440 | tf_op jit(solution)/shard_map/ppermute | solution.py:378
  98.3 2.7 %collective-permute-start.26 = (bf16[512,512]{1,0:T(8,128)(2,1)S(1)}, bf16[512,512]{1,0:T(8,128)(2,1)S(1)}, u32[]{:S(2)}, u32[]{:S(2)}) collective-permute-start(bf16[512,512]{1,0:T(8,128)(2,1)S(1)} %shard_map.98), channel_id=1, source_target_pairs={{0,1},{8,9},{16,17},{24,25},{32,33},{40,41},{48,49},{56,57},{2,3},... | collective-permute-start | bytes 1572872 | tf_op jit(solution)/shard_map/ppermute | solution.py:378
  101.0 1.7 %collective-permute-done.29.refs_3_ = bf16[512,256]{1,0:T(8,128)(2,1)S(1)} collective-permute-done((bf16[512,256]{1,0:T(8,128)(2,1)S(1)}, bf16[512,256]{1,0:T(8,128)(2,1)S(1)}, u32[]{:S(2)}, u32[]{:S(2)}) %collective-permute-start.29) | collective-permute-done | bytes 262176 | tf_op jit(solution)/shard_map/ppermute | solution.py:378
  103.6 2.8 %collective-permute-start.30 = (bf16[512,512]{1,0:T(8,128)(2,1)S(1)}, bf16[512,512]{1,0:T(8,128)(2,1)S(1)}, u32[]{:S(2)}, u32[]{:S(2)}) collective-permute-start(bf16[512,512]{1,0:T(8,128)(2,1)S(1)} %shard_map.100), channel_id=1, source_target_pairs={{0,1},{8,9},{16,17},{24,25},{32,33},{40,41},{48,49},{56,57},{2,3},... | collective-permute-start | bytes 1572872 | tf_op jit(solution)/shard_map/ppermute | solution.py:378
  108.3 6.3 %collective-permute-done.26.other0 = bf16[512,512]{1,0:T(8,128)(2,1)S(1)} collective-permute-done((bf16[512,512]{1,0:T(8,128)(2,1)S(1)}, bf16[512,512]{1,0:T(8,128)(2,1)S(1)}, u32[]{:S(2)}, u32[]{:S(2)}) %collective-permute-start.26) | collective-permute-done | bytes 524320 | tf_op jit(solution)/shard_map/ppermute | solution.py:378
  114.6 8.4 %collective-permute-done.30.other1 = bf16[512,512]{1,0:T(8,128)(2,1)S(1)} collective-permute-done((bf16[512,512]{1,0:T(8,128)(2,1)S(1)}, bf16[512,512]{1,0:T(8,128)(2,1)S(1)}, u32[]{:S(2)}, u32[]{:S(2)}) %collective-permute-start.30) | collective-permute-done | bytes 524320 | tf_op jit(solution)/shard_map/ppermute | solution.py:378
  123.0 1.7 %shard_map.102 = bf16[1024,512]{1,0:T(8,128)(2,1)} custom-call(s32[32]{0:T(128)S(1)} %copy-done.3, f32[512,512]{1,0:T(8,128)S(1)} %shard_map.99.own0, bf16[512,512]{1,0:T(8,128)(2,1)S(1)} %collective-permute-done.26.other0, f32[512,512]{1,0:T(8,128)S(1)} %shard_map.101.own1, bf16[512,512]{1,0:T(8,128)(2,1)S(1)} %collective-permute-done.30.other1), custom_call_target="tpu_custom_call" | custom-call | flops 524288 | bytes 4194304 | tf_op jit(solution)/shard_map/pallas_call | solution.py:346
  (57 shorter events, 17.8 us)
Async XLA Ops:
  0.0 23.2 %copy-start.3 = (s32[32]{0:T(128)S(1)}, s32[32]{0:T(128)}, u32[]{:S(2)}) copy-start(s32[32]{0:T(128)} %order_ref.15) | copy-start | bytes 388
  10.2 12.0 %collective-permute-start.6 = (bf16[2048,128]{1,0:T(8,128)(2,1)}, bf16[2048,128]{1,0:T(8,128)(2,1)}, u32[]{:S(2)}, u32[]{:S(2)}) collective-permute-start(bf16[2048,128]{1,0:T(8,128)(2,1)} %get-tuple-element.49.refs_0_), channel_id=1, source_target_pairs={{0,8},{8,0},{16,24},{24,16},{32,40},{40,32},{48,56},{56,48},{2,10}... | collective-permute-start | bytes 1572872 | tf_op jit(solution)/shard_map/ppermute | solution.py:378
  10.5 10.0 %collective-permute-start.3 = (bf16[256,512]{1,0:T(8,128)(2,1)S(1)}, bf16[256,512]{1,0:T(8,128)(2,1)S(1)}, u32[]{:S(2)}, u32[]{:S(2)}) collective-permute-start(bf16[256,512]{1,0:T(8,128)(2,1)S(1)} %get-tuple-element.95), channel_id=1, source_target_pairs={{0,2},{8,10},{16,18},{24,26},{32,34},{40,42},{48,50},{56,58},{2,4}... | collective-permute-start | bytes 786440 | tf_op jit(solution)/shard_map/ppermute | solution.py:378
  12.2 19.0 %collective-permute-start = (bf16[2048,128]{1,0:T(8,128)(2,1)}, bf16[2048,128]{1,0:T(8,128)(2,1)S(1)}, u32[]{:S(2)}, u32[]{:S(2)}) collective-permute-start(bf16[2048,128]{1,0:T(8,128)(2,1)} %get-tuple-element.49.refs_0_), channel_id=1, source_target_pairs={{0,16},{8,24},{16,32},{24,40},{32,48},{40,56},{48,0},{56,8},{2,18}... | collective-permute-start | bytes 1572872 | tf_op jit(solution)/shard_map/ppermute | solution.py:378
  14.2 17.1 %collective-permute-start.1 = (bf16[2048,128]{1,0:T(8,128)(2,1)}, bf16[2048,128]{1,0:T(8,128)(2,1)S(1)}, u32[]{:S(2)}, u32[]{:S(2)}) collective-permute-start(bf16[2048,128]{1,0:T(8,128)(2,1)} %get-tuple-element.49.refs_0_), channel_id=1, source_target_pairs={{0,64},{8,72},{16,80},{24,88},{32,96},{40,104},{48,112},{56,120},{... | collective-permute-start | bytes 1572872 | tf_op jit(solution)/shard_map/ppermute | solution.py:378
  15.7 15.6 %collective-permute-start.2 = (bf16[2048,128]{1,0:T(8,128)(2,1)}, bf16[2048,128]{1,0:T(8,128)(2,1)S(1)}, u32[]{:S(2)}, u32[]{:S(2)}) collective-permute-start(bf16[2048,128]{1,0:T(8,128)(2,1)} %get-tuple-element.49.refs_0_), channel_id=1, source_target_pairs={{0,48},{8,56},{16,0},{24,8},{32,16},{40,24},{48,32},{56,40},{2,50}... | collective-permute-start | bytes 1572872 | tf_op jit(solution)/shard_map/ppermute | solution.py:378
  20.5 9.2 %collective-permute-start.4 = (bf16[256,512]{1,0:T(8,128)(2,1)S(1)}, bf16[256,512]{1,0:T(8,128)(2,1)S(1)}, u32[]{:S(2)}, u32[]{:S(2)}) collective-permute-start(bf16[256,512]{1,0:T(8,128)(2,1)S(1)} %get-tuple-element.94), channel_id=1, source_target_pairs={{0,6},{8,14},{16,22},{24,30},{32,38},{40,46},{48,54},{56,62},{2,0}... | collective-permute-start | bytes 786440 | tf_op jit(solution)/shard_map/ppermute | solution.py:378
  22.3 9.0 %collective-permute-start.5 = (bf16[256,512]{1,0:T(8,128)(2,1)S(1)}, bf16[256,512]{1,0:T(8,128)(2,1)S(1)}, u32[]{:S(2)}, u32[]{:S(2)}) collective-permute-start(bf16[256,512]{1,0:T(8,128)(2,1)S(1)} %get-tuple-element.93), channel_id=1, source_target_pairs={{0,4},{8,12},{16,20},{24,28},{32,36},{40,44},{48,52},{56,60},{2,6}... | collective-permute-start | bytes 786440 | tf_op jit(solution)/shard_map/ppermute | solution.py:378
  31.3 4.7 %collective-permute-start.10 = (bf16[2048,128]{1,0:T(8,128)(2,1)S(1)}, bf16[2048,128]{1,0:T(8,128)(2,1)S(1)}, u32[]{:S(2)}, u32[]{:S(2)}) collective-permute-start(bf16[2048,128]{1,0:T(8,128)(2,1)S(1)} %collective-permute-done.refs_0_), channel_id=1, source_target_pairs={{0,8},{8,0},{16,24},{24,16},{32,40},{40,32},{48,56},{56,48},{2,10}... | collective-permute-start | bytes 1572872 | tf_op jit(solution)/shard_map/ppermute | solution.py:378
  31.4 6.1 %collective-permute-start.11 = (bf16[2048,128]{1,0:T(8,128)(2,1)S(1)}, bf16[2048,128]{1,0:T(8,128)(2,1)S(1)}, u32[]{:S(2)}, u32[]{:S(2)}) collective-permute-start(bf16[2048,128]{1,0:T(8,128)(2,1)S(1)} %collective-permute-done.2.refs_2_), channel_id=1, source_target_pairs={{0,8},{8,0},{16,24},{24,16},{32,40},{40,32},{48,56},{56,48},{2,10}... | collective-permute-start | bytes 1572872 | tf_op jit(solution)/shard_map/ppermute | solution.py:378
  31.9 5.7 %collective-permute-start.12 = (bf16[2048,128]{1,0:T(8,128)(2,1)S(1)}, bf16[2048,128]{1,0:T(8,128)(2,1)S(1)}, u32[]{:S(2)}, u32[]{:S(2)}) collective-permute-start(bf16[2048,128]{1,0:T(8,128)(2,1)S(1)} %collective-permute-done.1.refs_4_), channel_id=1, source_target_pairs={{0,8},{8,0},{16,24},{24,16},{32,40},{40,32},{48,56},{56,48},{2,10}... | collective-permute-start | bytes 1572872 | tf_op jit(solution)/shard_map/ppermute | solution.py:378
  32.0 16.5 %collective-permute-start.7 = (bf16[2048,128]{1,0:T(8,128)(2,1)S(1)}, bf16[2048,128]{1,0:T(8,128)(2,1)S(1)}, u32[]{:S(2)}, u32[]{:S(2)}) collective-permute-start(bf16[2048,128]{1,0:T(8,128)(2,1)S(1)} %collective-permute-done.refs_0_), channel_id=1, source_target_pairs={{0,16},{8,24},{16,32},{24,40},{32,48},{40,56},{48,0},{56,8},{2,18}... | collective-permute-start | bytes 1572872 | tf_op jit(solution)/shard_map/ppermute | solution.py:378
  33.9 14.6 %collective-permute-start.8 = (bf16[2048,128]{1,0:T(8,128)(2,1)S(1)}, bf16[2048,128]{1,0:T(8,128)(2,1)S(1)}, u32[]{:S(2)}, u32[]{:S(2)}) collective-permute-start(bf16[2048,128]{1,0:T(8,128)(2,1)S(1)} %collective-permute-done.1.refs_4_), channel_id=1, source_target_pairs={{0,48},{8,56},{16,0},{24,8},{32,16},{40,24},{48,32},{56,40},{2,50}... | collective-permute-start | bytes 1572872 | tf_op jit(solution)/shard_map/ppermute | solution.py:378
  36.0 14.0 %collective-permute-start.9 = (bf16[2048,128]{1,0:T(8,128)(2,1)S(1)}, bf16[2048,128]{1,0:T(8,128)(2,1)S(1)}, u32[]{:S(2)}, u32[]{:S(2)}) collective-permute-start(bf16[2048,128]{1,0:T(8,128)(2,1)S(1)} %collective-permute-done.refs_0_), channel_id=1, source_target_pairs={{0,64},{8,72},{16,80},{24,88},{32,96},{40,104},{48,112},{56,120},{... | collective-permute-start | bytes 1572872 | tf_op jit(solution)/shard_map/ppermute | solution.py:378
  50.0 2.3 %collective-permute-start.14 = (bf16[2048,128]{1,0:T(8,128)(2,1)S(1)}, bf16[2048,128]{1,0:T(8,128)(2,1)S(1)}, u32[]{:S(2)}, u32[]{:S(2)}) collective-permute-start(bf16[2048,128]{1,0:T(8,128)(2,1)S(1)} %collective-permute-done.7.refs_0_.refs_2_), channel_id=1, source_target_pairs={{0,8},{8,0},{16,24},{24,16},{32,40},{40,32},{48,56},{56,48},{2,10}... | collective-permute-start | bytes 1572872 | tf_op jit(solution)/shard_map/ppermute | solution.py:378
  50.7 2.3 %collective-permute-start.15 = (bf16[2048,128]{1,0:T(8,128)(2,1)S(1)}, bf16[2048,128]{1,0:T(8,128)(2,1)S(1)}, u32[]{:S(2)}, u32[]{:S(2)}) collective-permute-start(bf16[2048,128]{1,0:T(8,128)(2,1)S(1)} %collective-permute-done.8.refs_2_.refs_4_), channel_id=1, source_target_pairs={{0,8},{8,0},{16,24},{24,16},{32,40},{40,32},{48,56},{56,48},{2,10}... | collective-permute-start | bytes 1572872 | tf_op jit(solution)/shard_map/ppermute | solution.py:378
  50.8 2.9 %collective-permute-start.16 = (bf16[2048,128]{1,0:T(8,128)(2,1)S(1)}, bf16[2048,128]{1,0:T(8,128)(2,1)S(1)}, u32[]{:S(2)}, u32[]{:S(2)}) collective-permute-start(bf16[2048,128]{1,0:T(8,128)(2,1)S(1)} %collective-permute-done.9.refs_4_.refs_6_), channel_id=1, source_target_pairs={{0,8},{8,0},{16,24},{24,16},{32,40},{40,32},{48,56},{56,48},{2,10}... | collective-permute-start | bytes 1572872 | tf_op jit(solution)/shard_map/ppermute | solution.py:378
  51.3 9.6 %collective-permute-start.13 = (bf16[1024,128]{1,0:T(8,128)(2,1)S(1)}, bf16[1024,128]{1,0:T(8,128)(2,1)S(1)}, u32[]{:S(2)}, u32[]{:S(2)}) collective-permute-start(bf16[1024,128]{1,0:T(8,128)(2,1)S(1)} %slice.6), channel_id=1, source_target_pairs={{0,16},{8,24},{16,32},{24,40},{32,48},{40,56},{48,0},{56,8},{2,18}... | collective-permute-start | bytes 786440 | tf_op jit(solution)/shard_map/ppermute | solution.py:378
  60.9 2.8 %collective-permute-start.17 = (bf16[1024,128]{1,0:T(8,128)(2,1)S(1)}, bf16[1024,128]{1,0:T(8,128)(2,1)S(1)}, u32[]{:S(2)}, u32[]{:S(2)}) collective-permute-start(bf16[1024,128]{1,0:T(8,128)(2,1)S(1)} %collective-permute-done.13.refs_0_), channel_id=1, source_target_pairs={{0,8},{8,0},{16,24},{24,16},{32,40},{40,32},{48,56},{56,48},{2,10}... | collective-permute-start | bytes 786440 | tf_op jit(solution)/shard_map/ppermute | solution.py:378
  62.5 10.2 %collective-permute-start.18 = (bf16[1024,128]{1,0:T(8,128)(2,1)S(1)}, bf16[1024,128]{1,0:T(8,128)(2,1)S(1)}, u32[]{:S(2)}, u32[]{:S(2)}) collective-permute-start(bf16[1024,128]{1,0:T(8,128)(2,1)S(1)} %slice.7), channel_id=1, source_target_pairs={{0,48},{8,56},{16,0},{24,8},{32,16},{40,24},{48,32},{56,40},{2,50}... | collective-permute-start | bytes 786440 | tf_op jit(solution)/shard_map/ppermute | solution.py:378
  65.0 12.5 %collective-permute-start.19 = (bf16[512,256]{1,0:T(8,128)(2,1)S(1)}, bf16[512,256]{1,0:T(8,128)(2,1)S(1)}, u32[]{:S(2)}, u32[]{:S(2)}) collective-permute-start(bf16[512,256]{1,0:T(8,128)(2,1)S(1)} %shard_map.95.refs_0_), channel_id=1, source_target_pairs={{0,2},{8,10},{16,18},{24,26},{32,34},{40,42},{48,50},{56,58},{2,4}... | collective-permute-start | bytes 786440 | tf_op jit(solution)/shard_map/ppermute | solution.py:378
  77.5 2.6 %collective-permute-start.22 = (bf16[1024,128]{1,0:T(8,128)(2,1)S(1)}, bf16[1024,128]{1,0:T(8,128)(2,1)S(1)}, u32[]{:S(2)}, u32[]{:S(2)}) collective-permute-start(bf16[1024,128]{1,0:T(8,128)(2,1)S(1)} %collective-permute-done.18.refs_0_), channel_id=1, source_target_pairs={{0,8},{8,0},{16,24},{24,16},{32,40},{40,32},{48,56},{56,48},{2,10}... | collective-permute-start | bytes 786440 | tf_op jit(solution)/shard_map/ppermute | solution.py:378
  77.6 8.7 %collective-permute-start.20 = (bf16[512,256]{1,0:T(8,128)(2,1)S(1)}, bf16[512,256]{1,0:T(8,128)(2,1)S(1)}, u32[]{:S(2)}, u32[]{:S(2)}) collective-permute-start(bf16[512,256]{1,0:T(8,128)(2,1)S(1)} %shard_map.95.refs_0_), channel_id=1, source_target_pairs={{0,6},{8,14},{16,22},{24,30},{32,38},{40,46},{48,54},{56,62},{2,0}... | collective-permute-start | bytes 786440 | tf_op jit(solution)/shard_map/ppermute | solution.py:378
  79.5 9.4 %collective-permute-start.21 = (bf16[512,256]{1,0:T(8,128)(2,1)S(1)}, bf16[512,256]{1,0:T(8,128)(2,1)S(1)}, u32[]{:S(2)}, u32[]{:S(2)}) collective-permute-start(bf16[512,256]{1,0:T(8,128)(2,1)S(1)} %collective-permute-done.19.refs_1_), channel_id=1, source_target_pairs={{0,2},{8,10},{16,18},{24,26},{32,34},{40,42},{48,50},{56,58},{2,4}... | collective-permute-start | bytes 786440 | tf_op jit(solution)/shard_map/ppermute | solution.py:378
  79.6 9.9 %collective-permute-start.23 = (bf16[256,512]{1,0:T(8,128)(2,1)S(1)}, bf16[256,512]{1,0:T(8,128)(2,1)S(1)}, u32[]{:S(2)}, u32[]{:S(2)}) collective-permute-start(bf16[256,512]{1,0:T(8,128)(2,1)S(1)} %collective-permute-done.3.refs_5_), channel_id=1, source_target_pairs={{0,8},{8,0},{16,24},{24,16},{32,40},{40,32},{48,56},{56,48},{2,10}... | collective-permute-start | bytes 786440 | tf_op jit(solution)/shard_map/ppermute | solution.py:378
  79.6 9.9 %collective-permute-start.24 = (bf16[256,512]{1,0:T(8,128)(2,1)S(1)}, bf16[256,512]{1,0:T(8,128)(2,1)S(1)}, u32[]{:S(2)}, u32[]{:S(2)}) collective-permute-start(bf16[256,512]{1,0:T(8,128)(2,1)S(1)} %collective-permute-done.4.refs_6_), channel_id=1, source_target_pairs={{0,8},{8,0},{16,24},{24,16},{32,40},{40,32},{48,56},{56,48},{2,10}... | collective-permute-start | bytes 786440 | tf_op jit(solution)/shard_map/ppermute | solution.py:378
  80.1 9.4 %collective-permute-start.25 = (bf16[256,512]{1,0:T(8,128)(2,1)S(1)}, bf16[256,512]{1,0:T(8,128)(2,1)S(1)}, u32[]{:S(2)}, u32[]{:S(2)}) collective-permute-start(bf16[256,512]{1,0:T(8,128)(2,1)S(1)} %collective-permute-done.5.refs_7_), channel_id=1, source_target_pairs={{0,8},{8,0},{16,24},{24,16},{32,40},{40,32},{48,56},{56,48},{2,10}... | collective-permute-start | bytes 786440 | tf_op jit(solution)/shard_map/ppermute | solution.py:378
  86.2 9.1 %collective-permute-start.27 = (bf16[512,256]{1,0:T(8,128)(2,1)S(1)}, bf16[512,256]{1,0:T(8,128)(2,1)S(1)}, u32[]{:S(2)}, u32[]{:S(2)}) collective-permute-start(bf16[512,256]{1,0:T(8,128)(2,1)S(1)} %shard_map.97.refs_0_), channel_id=1, source_target_pairs={{0,2},{8,10},{16,18},{24,26},{32,34},{40,42},{48,50},{56,58},{2,4}... | collective-permute-start | bytes 786440 | tf_op jit(solution)/shard_map/ppermute | solution.py:378
  88.9 7.3 %collective-permute-start.28 = (bf16[512,256]{1,0:T(8,128)(2,1)S(1)}, bf16[512,256]{1,0:T(8,128)(2,1)S(1)}, u32[]{:S(2)}, u32[]{:S(2)}) collective-permute-start(bf16[512,256]{1,0:T(8,128)(2,1)S(1)} %shard_map.97.refs_0_), channel_id=1, source_target_pairs={{0,6},{8,14},{16,22},{24,30},{32,38},{40,46},{48,54},{56,62},{2,0}... | collective-permute-start | bytes 786440 | tf_op jit(solution)/shard_map/ppermute | solution.py:378
  96.2 6.4 %collective-permute-start.29 = (bf16[512,256]{1,0:T(8,128)(2,1)S(1)}, bf16[512,256]{1,0:T(8,128)(2,1)S(1)}, u32[]{:S(2)}, u32[]{:S(2)}) collective-permute-start(bf16[512,256]{1,0:T(8,128)(2,1)S(1)} %collective-permute-done.28.refs_2_), channel_id=1, source_target_pairs={{0,6},{8,14},{16,22},{24,30},{32,38},{40,46},{48,54},{56,62},{2,0}... | collective-permute-start | bytes 786440 | tf_op jit(solution)/shard_map/ppermute | solution.py:378
  98.3 16.4 %collective-permute-start.26 = (bf16[512,512]{1,0:T(8,128)(2,1)S(1)}, bf16[512,512]{1,0:T(8,128)(2,1)S(1)}, u32[]{:S(2)}, u32[]{:S(2)}) collective-permute-start(bf16[512,512]{1,0:T(8,128)(2,1)S(1)} %shard_map.98), channel_id=1, source_target_pairs={{0,1},{8,9},{16,17},{24,25},{32,33},{40,41},{48,49},{56,57},{2,3},... | collective-permute-start | bytes 1572872 | tf_op jit(solution)/shard_map/ppermute | solution.py:378
  103.6 19.4 %collective-permute-start.30 = (bf16[512,512]{1,0:T(8,128)(2,1)S(1)}, bf16[512,512]{1,0:T(8,128)(2,1)S(1)}, u32[]{:S(2)}, u32[]{:S(2)}) collective-permute-start(bf16[512,512]{1,0:T(8,128)(2,1)S(1)} %shard_map.100), channel_id=1, source_target_pairs={{0,1},{8,9},{16,17},{24,25},{32,33},{40,41},{48,49},{56,57},{2,3},... | collective-permute-start | bytes 1572872 | tf_op jit(solution)/shard_map/ppermute | solution.py:378
  (4 other events, 59.3 us)
